TPU v7x, 512 devices: a whole 4x8x8 slice. The times are simulated.
512 devices in a mesh: shot: 128 (over x, z, y_hi, core), freq: 4 (over y_lo).
Axes of the slice: x: 4, y: 8 (y_hi: 2, y_lo: 4; y = y_hi * 4 + y_lo), z: 8, core: 2. Of those that a mesh axis runs over, the one named last changes fastest.
Arguments:
- traces: float32 [384, 256, 1024], P('shot', None, 'freq'), may hold values from -6 to 6
- live_mask: int32 [384, 256], P('shot'), may hold values 0 or 1
- offset_bin: int32 [384, 256, 1], P('shot'), may hold values from 0 to 511; in each aligned block of 768 rows (0 to 767, 768 to 1535, ..., all dimensions but the last counted through in order) at most 2 rows name the same one
- surface: float32 [2048, 256, 512], P('shot', None, 'freq'), may hold values from -2.5 to 2.5
- block_owner: int32 [2], replicated, may hold values from 0 to 127
- point_column: int32 [2, 16], replicated, may hold values from 0 to 255
- filters: float32 [512, 31], P('shot'), may hold values from -1 to 1
Outputs:
- primaries: float32 [512, 256, 1024], P('shot', None, 'freq')
Inputs may be any that keep to these rules, and one draw needn't show every extreme that they name: `offset_bin`: among the traces of one group of 3 consecutive shots (the rows of one device) no bin holds more than 2 traces, and in every draw some group has a bin with exactly 2; every bin holds some trace.
All inputs are finite; a program needn't handle non-finite values. No bound on the sum of `live_mask` on one device may be relied on, other than what follows from the above.
Results may differ from a plain program's by a relative error of at most 0.0003.
Values sent between devices are 32-bit elements; how exact they have to be, the bound alone decides.
A program may use at most 64 MiB of HBM per device.

v0:
```python
import math

import jax
import jax.numpy as jnp
from jax import lax
from jax.sharding import PartitionSpec as P

NT = 1024
NF = 256
TAPS = 31
POINTS_BLK = 16
STEPS = 2


FULL_PRECISION = lax.Precision.HIGHEST


def with_halo(cells, sides, width):
    for axis, dim in sides:
        count = lax.axis_size(axis)
        ends = count - 1
        head = lax.slice_in_dim(cells, 0, width, axis=dim)
        tail = lax.slice_in_dim(cells, cells.shape[dim] - width, cells.shape[dim], axis=dim)
        cells = jnp.concatenate(
            [
                lax.ppermute(tail, axis, [(i, (i + 1) % count) for i in range(ends)]),
                cells,
                lax.ppermute(head, axis, [((i + 1) % count, i) for i in range(ends)]),
            ],
            axis=dim,
        )
    return cells


def broadcast(value, axis, source):
    kept = jnp.where(lax.axis_index(axis) == source, value, 0).astype(value.dtype)
    return lax.psum(kept, axis)


def wave_table(time_ids, comp_ids, band_width, period):
    mode_ids = comp_ids // (2 * band_width) * band_width + comp_ids % band_width
    phase_ids = (mode_ids[None, :] + 1) * time_ids[:, None] % period
    angles = phase_ids.astype(jnp.float32) * (2.0 * math.pi / period)
    real_part = comp_ids % (2 * band_width) < band_width
    return jnp.where(real_part[None, :], jnp.cos(angles), -jnp.sin(angles))


def cross_mix(left_side, right_side):
    return jnp.einsum("bsj,jrb->srb", left_side, right_side, precision=FULL_PRECISION)


def shifted_sum(widened, tap_table, out_width):
    half_span = (tap_table.shape[-1] - 1) // 2
    summed = jnp.zeros(widened.shape[:-1] + (out_width,), jnp.float32)
    for tap_index in range(tap_table.shape[-1]):
        offset_start = 2 * half_span - tap_index
        window = lax.slice_in_dim(
            widened, offset_start, offset_start + out_width, axis=widened.ndim - 1
        )
        summed = summed + tap_table[..., tap_index : tap_index + 1] * window
    return summed


def widened_rims(values):
    half_span = (TAPS - 1) // 2
    return with_halo(values, (("freq", 2),), half_span)


def pack_rows(values, slot_ids, total_slots):
    return jnp.zeros((total_slots, values.shape[-1]), jnp.float32).at[slot_ids].set(values)


def on_device(traces, live_mask, offset_bin, surface, block_owner, point_column, filters):
    shots_here, receivers, quarter = traces.shape
    freq_count = lax.axis_size("freq")
    shot_count = lax.axis_size("shot")
    band_width = NF // freq_count
    rows_here = shots_here * receivers
    bins_total = filters.shape[0] * shot_count
    most_slots = max(2, 3 * rows_here // (2 * bins_total))
    total_slots = bins_total * most_slots
    live_rows = live_mask.astype(jnp.float32)[:, :, None]
    live_traces = traces * live_rows
    columns = point_column.reshape(-1)
    picked = jnp.take(live_traces, columns, axis=1).reshape(shots_here * columns.shape[0], quarter)
    freq_index = lax.axis_index("freq")
    time_ids = freq_index * quarter + jnp.arange(quarter)
    band_ids = freq_index * 2 * band_width + jnp.arange(2 * band_width)
    wave_rows = wave_table(
        time_ids, jnp.arange(2 * band_width * lax.axis_size("freq")), band_width, NT
    )
    spectra = lax.psum_scatter(
        lax.dot_general(wave_rows, picked, (((0,), (1,)), ((), ())), precision=FULL_PRECISION),
        "freq",
        scatter_dimension=0,
        tiled=True,
    )
    spectra = spectra.reshape(2 * band_width, shots_here, columns.shape[0])
    real_sum = jnp.zeros((shots_here, receivers, band_width), jnp.float32)
    imag_sum = jnp.zeros((shots_here, receivers, band_width), jnp.float32)
    for step_index in range(STEPS):
        surface_part = broadcast(surface, "shot", block_owner[step_index])
        point_spectra = spectra[:, :, step_index * POINTS_BLK : (step_index + 1) * POINTS_BLK]
        data_real = point_spectra[:band_width]
        data_imag = point_spectra[band_width:]
        surf_real = surface_part[:, :, :band_width]
        surf_imag = surface_part[:, :, band_width:]
        real_sum = real_sum + (cross_mix(data_real, surf_real) - cross_mix(data_imag, surf_imag))
        imag_sum = imag_sum + (cross_mix(data_real, surf_imag) + cross_mix(data_imag, surf_real))
    prediction = jnp.concatenate([real_sum, imag_sum], axis=2).reshape(rows_here, 2 * band_width)
    inverse = wave_table(jnp.arange(NT), band_ids, band_width, NT).T * (2.0 / NT)
    partial_value = jnp.dot(prediction, inverse, precision=FULL_PRECISION)
    multiples = lax.psum_scatter(partial_value, "freq", scatter_dimension=1, tiled=True)
    multiples = multiples.reshape(shots_here, receivers, quarter) * live_rows
    bins_flat = offset_bin.reshape(rows_here)
    order_ids = jnp.arange(rows_here)
    earlier = (bins_flat[:, None] == bins_flat[None, :]) & (order_ids[None, :] < order_ids[:, None])
    rank_ids = jnp.sum(earlier.astype(jnp.int32), axis=1)
    slot_ids = bins_flat * most_slots + rank_ids
    every_filter = lax.all_gather(filters, "shot", axis=0, tiled=True)
    trace_taps = jnp.take(every_filter, bins_flat, axis=0).reshape(
        shots_here, receivers, every_filter.shape[1]
    )
    widened = widened_rims(multiples)
    cleaned = live_traces - shifted_sum(widened, trace_taps, quarter)
    cleaned_slots = pack_rows(cleaned.reshape(rows_here, quarter), slot_ids, total_slots)
    cleaned_slots = cleaned_slots.reshape(bins_total, most_slots, quarter)
    return lax.all_to_all(cleaned_slots, "shot", split_axis=0, concat_axis=1, tiled=True)


def solution(mesh):
    return jax.shard_map(
        on_device,
        mesh=mesh,
        in_specs=(
            P("shot", None, "freq"),
            P("shot", None),
            P("shot", None, None),
            P("shot", None, "freq"),
            P(),
            P(),
            P("shot", None),
        ),
        out_specs=P("shot", None, "freq"),
        check_vma=False,
    )
```

profile of v0, /device:TPU:1, one launch (start us, length us, event | category | flops | bytes accessed | tf_op | source)
XLA Modules:
  0.0 1985.6 jit_solution(8417712239140082174)
XLA Ops:
  9.8 1.8 copy_multiply_fusion.1
  12.4 3.3 fusion.109
  17.6 2.2 copy.152
  19.9 2.6 broadcast_select_fusion.1
  22.8 23.6 %reduce-scatter.3.cloned.1.call-done = f32[128,96]{0,1:T(8,128)} async-done(((f32[512,96]{0,1:T(8,128)}), f32[128,96]{0,1:T(8,128)}) %reduce-scatter.3.cloned.1.call-update) | async-done | bytes 49168 | tf_op jit(solution)/shard_map/reduce_scatter | solution.py:92
  47.7 1551.4 %all-reduce.3.cloned.1.call-done = (f32[16,256,128]{1,0,2:T(8,128)}, f32[16,256,128]{1,0,2:T(8,128)}) async-done(((f32[16,256,128]{1,0,2:T(8,128)}, f32[16,256,128]{1,0,2:T(8,128)}), (f32[16,256,128]{1,0,2:T(8,128)}, f32[16,256,128]{1,0,2:T(8,128)})) %all-reduce.3.cloned.1.call-update) | async-done | bytes 4194320 | tf_op jit(solution)/shard_map/psum | solution.py:37
  1599.1 2.1 fusion.170
  1607.4 6.2 fusion.100
  1614.4 221.0 %all-gather = f32[128,4,31]{2,1,0:T(4,128)S(1)} all-gather(f32[1,4,31]{2,1,0:T(4,128)S(1)} %bitcast.117), channel_id=1, replica_groups=mesh['shot'=128,'freq'=4] {'shot'}, dimensions={0}, use_global_device_ids=true | all-gather | bytes 63984 | tf_op jit(solution)/shard_map/all_gather | solution.py:120
  1836.3 1.6 gather_fusion
  1838.8 1.8 copy_multiply_fusion
  1840.6 1.3 fusion.166
  1841.9 1.3 collective-permute-start
  1843.2 8.5 collective-permute-start.1
  1854.7 1.5 copy.184
  1856.1 1.5 copy.185
  1857.6 1.5 copy.186
  1862.2 1.4 copy.161
  1863.7 1.5 copy.162
  1865.2 1.5 copy.163
  1866.6 1.5 copy.164
  1868.1 1.5 copy.165
  1869.6 1.5 copy.166
  1871.0 1.5 copy.167
  1872.5 1.5 copy.168
  1873.9 1.5 copy.169
  1875.4 1.5 copy.170
  1876.9 1.5 copy.171
  1878.4 1.5 copy.172
  1879.8 54.1 %fusion.9 = f32[3,256,256]{2,0,1:T(4,128)S(1)} fusion(f32[3,256,256]{2,0,1:T(4,128)S(1)} %copy_multiply_fusion, f32[3,256,15]{2,0,1:T(4,128)} %collective-permute-done.1, f32[3,256,15]{2,0,1:T(4,128)} %collective-permute-done, f32[3,256]{0,1:T(8,128)} %copy.190, f32[3,256]{0,1:T(8,128)} %copy.189, f32[3,256]{0,1:T(8,128)} %copy.188, f32[3,256]{0,1:T(8,128)} %copy.187, ...), kind=kLoop, calls=%fused_computation.74 | loop fusion | flops 18284544 | bytes 2549760 | tf_op jit(solution)/shard_map/sub | solution.py:125
  1934.1 5.9 scatter_custom_fusion
  1940.6 36.1 %all_to_all.18 = f32[512,2,256]{2,1,0:T(2,128)S(1)} all-to-all(f32[512,2,256]{2,1,0:T(2,128)S(1)} %reshape.223), channel_id=1, replica_groups=mesh['shot'=128,'freq'=4] {'shot'}, dimensions={0} | all-to-all | bytes 2097152 | tf_op jit(solution)/shard_map/all_to_all | solution.py:128
  (83 shorter events, 22.5 us)
Async XLA Ops:
  7.4 39.0 %reduce-scatter.3.cloned.1.call-start = ((), (), s32[]{:S(2)}) async-start(), calls=%async_computation.3 | async-start | bytes 245760 | tf_op jit(solution)/shard_map/reduce_scatter | solution.py:92
  11.5 4.2 copy-start.5
  15.7 1583.4 %all-reduce.3.cloned.1.call-start = ((), (), s32[]{:S(2)}) async-start(), calls=%async_computation.5 | async-start | bytes 8388608 | tf_op jit(solution)/shard_map/psum | solution.py:37
  22.5 1816.3 %reduce-scatter.5.cloned.1.call-start = ((), (), s32[]{:S(2)}) async-start(), calls=%async_computation.4 | async-start | bytes 3932160 | tf_op jit(solution)/shard_map/reduce_scatter | solution.py:113
  1599.1 2.1 copy-start.1
  1601.2 1.6 copy-start
  1613.7 0.7 copy-start.3
  1613.7 0.7 copy-start.4
  1841.9 38.0 %collective-permute-start = (f32[3,256,15]{2,0,1:T(4,128)}, f32[3,256,15]{2,0,1:T(4,128)}, u32[]{:S(2)}, u32[]{:S(2)}) collective-permute-start(f32[3,256,15]{2,0,1:T(4,128)} %get-tuple-element.11), channel_id=1, source_target_pairs={{1,0},{2,1},{3,2},{5,4},{6,5},{7,6},{9,8},{10,9},{11,10},{13,12},{... | collective-permute-start | bytes 138248 | tf_op jit(solution)/shard_map/ppermute | solution.py:28
  1843.2 36.7 %collective-permute-start.1 = (f32[3,256,15]{2,0,1:T(4,128)}, f32[3,256,15]{2,0,1:T(4,128)}, u32[]{:S(2)}, u32[]{:S(2)}) collective-permute-start(f32[3,256,15]{2,0,1:T(4,128)} %get-tuple-element.12), channel_id=1, source_target_pairs={{0,1},{1,2},{2,3},{4,5},{5,6},{6,7},{8,9},{9,10},{10,11},{12,13},{... | collective-permute-start | bytes 138248 | tf_op jit(solution)/shard_map/ppermute | solution.py:26
  1852.2 27.6 %copy-start.2 = (f32[3,256,256]{2,1,0:T(8,128)S(1)}, f32[3,256,256]{2,1,0:T(8,128)}, u32[]{:S(2)}) copy-start(f32[3,256,256]{2,1,0:T(8,128)} %param.7) | copy-start | bytes 2359300
Sparse Core Ops, SparseCore 0:
  15.8 30.5 reduce-scatter.2
  1613.8 62.7 reduce-scatter.4
Sparse Core Ops, SparseCore 1:
  22.6 1576.5 all-reduce.2
where the time goes:
time: 1990 us
  waiting for transfers between devices  1580 us (79%)
  blocking collectives  257 us (13%)
  other arithmetic  62.2 us (3%)
  local copies, waits for them, and re-layouts  48.2 us (2%)
    psum x1, waiting for transfers between devices, broadcast(): return lax.psum(kept, axis)  1550 us
    all_gather x1, blocking collectives, on_device(): every_filter = lax.all_gather(filters, 'shot', axis=0, tiled=True)  221 us
    sub x1, other arithmetic, on_device(): cleaned = live_traces - shifted_sum(widened, trace_taps, quarter)  54.1 us
  transfers between devices with their start and end apart: 5, of which 2 were waited for; matrix products, arithmetic and copies ran while one was open for 2% of the time, Pallas kernels for 0%

commit v1 on v0

v1 whole, which is shorter than its diff:
```python
import functools
import math

import jax
import jax.numpy as jnp
import numpy as np
from jax import lax
from jax.experimental import pallas as pl
from jax.experimental.pallas import tpu as pltpu
from jax.sharding import PartitionSpec as P

NT = 1024
NF = 256
TAPS = 31
POINTS_BLK = 16
STEPS = 2
NX, NZ, NH, NC = 4, 8, 2, 2
NQ = 4
BAND = NF // NQ
LANES = 2 * BAND
QUARTER = NT // NQ
R = 256
SHOTS = 3
ROWS = SHOTS * R
PIECES = NX * NC
CHUNKS = 4
SUB = 8
COLS = STEPS * POINTS_BLK
PAIR = POINTS_BLK // NZ
EDGE = (TAPS - 1) // 2
FULL = lax.Precision.HIGHEST
MESH = pl.DeviceIdType.MESH
F32 = jnp.float32


def tables():
    t = np.arange(NT)
    m = np.arange(NF) + 1
    phase = 2 * np.pi * ((m[:, None] * t[None, :]) % NT) / NT
    real = np.cos(phase).reshape(NQ, BAND, NT)
    imag = -np.sin(phase).reshape(NQ, BAND, NT)
    wave = np.concatenate([real, imag], axis=1).reshape(NQ * LANES, NT)
    forward = wave.T.reshape(NQ, QUARTER, NQ * LANES)
    synth = wave * (2.0 / NT)
    k = np.arange(64)
    u = np.arange(EDGE)
    turn = 2 * np.pi * ((u[:, None] * k[None, :]) % 64) / 64
    short = np.concatenate([np.cos(turn), -np.sin(turn)], axis=1)
    edge = np.zeros((NQ, NQ * LANES, 128))
    edge[0] = synth[:, NT - EDGE :] @ short
    edge[NQ - 1] = synth[:, :EDGE] @ short
    back = np.zeros((NQ, 128, QUARTER))

    def inverse(n):
        a = 2 * np.pi * ((k[:, None] * n[None, :]) % 64) / 64
        return -np.concatenate([np.cos(a), -np.sin(a)], axis=0) / 64

    back[0][:, :EDGE] = inverse(np.arange(2 * EDGE, 3 * EDGE))
    back[NQ - 1][:, QUARTER - EDGE :] = inverse(np.arange(EDGE))
    combine = np.concatenate(
        [synth.reshape(NQ * LANES, NQ, QUARTER).transpose(1, 0, 2), back], axis=1
    )
    i = np.arange(TAPS)
    lag = 2 * np.pi * (((i[:, None] - EDGE) * m[None, :]) % NT) / NT
    c, s = np.cos(lag).reshape(TAPS, NQ, BAND), np.sin(lag).reshape(TAPS, NQ, BAND)
    same = np.concatenate([c, c], axis=2).reshape(TAPS, NQ * LANES)
    cross = np.concatenate([s, -s], axis=2).reshape(TAPS, NQ * LANES)
    lag2 = 2 * np.pi * ((i[:, None] * k[None, :]) % 64) / 64
    same2 = np.concatenate([np.cos(lag2), np.cos(lag2)], axis=1)
    cross2 = np.concatenate([np.sin(lag2), -np.sin(lag2)], axis=1)
    taps = np.concatenate([same, same2, cross, cross2], axis=1)
    taps = np.concatenate([taps] * 4 + [np.zeros((4, taps.shape[1]))], axis=0)
    return [np.asarray(a, np.float32) for a in (forward, edge, combine, taps)]


FORWARD, EDGE_IN, COMBINE, TAP_TABLE = tables()


def place():
    d = lax.axis_index("shot")
    x, z = d // (NZ * NH * NC), d // (NH * NC) % NZ
    return x, z, d // NC % NH, d % NC, lax.axis_index("freq")


def shot_of(x, z, h, c):
    return ((x * NZ + z) * NH + h) * NC + c


def spread_kernel(
    traces, live, cols, wave, surface, weights, filt, bands, table,
    r1, m, r2, hown, hin, ag, specp, specr, specall, sa, sb, srot, pred, f1, f1c,
    s1s, s1r, s2s, s2r, hs, hr, gs, gr, bs, br, fs, fr,
    ps, pr, cs, cr, u1s, u1r, u2s, u2r, us, ur, own,
):
    x, z, h, c, f = place()
    mine = x * NC + c

    def dev_p(j):
        p = lax.rem(mine + j, PIECES)
        return p, (shot_of(p // NC, z, h, lax.rem(p, NC)), f)

    def dev_z(j):
        o = lax.rem(z + j, NZ)
        return o, (shot_of(x, o, h, c), f)

    def dev_f(j):
        o = lax.rem(f + j, NQ)
        return o, (shot_of(x, z, h, c), o)

    other_h = (shot_of(x, z, 1 - h, c), f)

    barrier = pltpu.get_barrier_semaphore()

    def greet(dev):
        pl.semaphore_signal(barrier, inc=1, device_id=dev, device_id_type=MESH)

    def each(count, fn):
        def body(j, _):
            fn(j)
            return 0

        lax.fori_loop(1, count, body, 0)

    each(PIECES, lambda j: greet(dev_p(j)[1]))
    each(NZ, lambda j: greet(dev_z(j)[1]))
    each(NQ, lambda j: greet(dev_f(j)[1]))
    greet(other_h)
    pl.semaphore_wait(barrier, PIECES - 1 + NZ - 1 + NQ - 1 + 1)

    def remote(src, dst, send, recv, dev):
        return pltpu.make_async_remote_copy(
            src_ref=src, dst_ref=dst, send_sem=send, recv_sem=recv,
            device_id=dev, device_id_type=MESH,
        )

    def first(k, j, at):
        p, dev = dev_p(j)
        src = surface.at[:, pl.ds(pl.multiple_of(p * (CHUNKS * SUB) + k * SUB, SUB), SUB), :]
        return remote(src, r1.at[k, at(p)], s1s.at[k, p], s1r.at[k, at(p)], dev)

    def second(k, j, at):
        o, dev = dev_z(j)
        return remote(
            m.at[k, :, pl.ds(o * PAIR, PAIR)], r2.at[k, at(o)], s2s.at[k, o], s2r.at[k, at(o)], dev
        )

    def third(k):
        return remote(hown.at[k], hin.at[k], hs.at[k], hr.at[k], other_h)

    def fourth(k, j, at):
        o, dev = dev_z(j)
        return remote(ag.at[k, z], ag.at[k, at(o)], gs.at[k, o], gr.at[k, at(o)], dev)

    def fifth(k, j, at):
        p, dev = dev_p(j)
        return remote(
            pred.at[p, :, k], bands.at[f, :, at(p), k], bs.at[k, p], br.at[k, at(p)], dev
        )

    def sixth(k, j, at):
        o, dev = dev_f(j)
        return remote(
            bands.at[f, :, :, k], bands.at[at(o), :, :, k], fs.at[k, o], fr.at[k, at(o)], dev
        )

    def spec_f(j, at):
        o, dev = dev_f(j)
        return remote(specp.at[o], specr.at[at(o)], ps.at[o], pr.at[at(o)], dev)

    def spec_p(j, at):
        p, dev = dev_p(j)
        return remote(specall.at[mine], specall.at[at(p)], cs.at[p], cr.at[at(p)], dev)

    def filt_p(j, at):
        p, dev = dev_p(j)
        return remote(filt, f1.at[at(p)], u1s.at[p], u1r.at[at(p)], dev)

    def filt_z(j, at):
        o, dev = dev_z(j)
        return remote(f1c, table.at[h, at(o)], u2s.at[o], u2r.at[at(o)], dev)

    def filt_h(at):
        return remote(table.at[h], table.at[at], us, ur, other_h)

    def to_p(p):
        return mine

    def to_z(o):
        return z

    def to_f(o):
        return f

    def here(o):
        return o

    each(PIECES, lambda j: filt_p(j, to_p).start())

    def start_first(k, _):
        each(PIECES, lambda j: first(k, j, to_p).start())
        return 0

    lax.fori_loop(0, CHUNKS, start_first, 0)

    def own_piece(k):
        src = surface.at[:, pl.ds(pl.multiple_of(mine * (CHUNKS * SUB) + k * SUB, SUB), SUB), :]
        return pltpu.make_async_copy(src, r1.at[k, mine], own.at[k])

    for k in range(CHUNKS):
        own_piece(k).start()

    at_point = lax.broadcasted_iota(jnp.int32, (COLS, R), 1) == cols[...]
    for s in range(SHOTS):
        pick = jnp.where(at_point, live[s : s + 1, :], 0.0)
        picked = jnp.dot(pick, traces[s], precision=FULL, preferred_element_type=F32)
        part = jnp.dot(picked, wave[...], precision=FULL, preferred_element_type=F32)
        for o in range(NQ):
            specp[o, s * COLS : (s + 1) * COLS, :] = part[:, o * LANES : (o + 1) * LANES]
    each(NQ, lambda j: spec_f(j, to_f).start())
    specr[f] = specp[f]

    f1[mine] = filt[...]
    each(PIECES, lambda j: filt_p(j, here).wait_recv())
    for p in range(PIECES):
        f1c[p : p + 1, :] = f1[p, 0:1, :]
    each(NZ, lambda j: filt_z(j, to_z).start())

    each(NQ, lambda j: spec_f(j, here).wait_recv())
    specall[mine] = specr[0] + specr[1] + specr[2] + specr[3]
    each(PIECES, lambda j: spec_p(j, to_p).start())

    table[h, z] = f1c[...]
    each(NZ, lambda j: filt_z(j, here).wait_recv())
    filt_h(h).start()

    each(PIECES, lambda j: spec_p(j, here).wait_recv())
    low = lax.broadcasted_iota(jnp.int32, (SHOTS * COLS, LANES), 1) < BAND

    def both(p, _):
        v = specall[p]
        w = pltpu.roll(v, BAND, 1)
        sa[p] = jnp.where(low, v, w)
        sb[p] = jnp.where(low, -w, v)
        return 0

    lax.fori_loop(0, PIECES, both, 0)

    def predict(k):
        each(NZ, lambda j: fourth(k, j, here).wait_recv())
        srot[...] = pltpu.roll(
            ag[k].reshape(NZ * STEPS * PAIR * SUB, LANES), BAND, 1
        ).reshape(NZ, STEPS, PAIR, SUB, LANES)

        def piece(p, _):
            totals = [jnp.zeros((SUB, LANES), F32) for _ in range(SHOTS)]
            for o in range(NZ):
                for b in range(STEPS):
                    for i in range(PAIR):
                        straight, turned = ag[k, o, b, i], srot[o, b, i]
                        for s in range(SHOTS):
                            row = s * COLS + b * POINTS_BLK + o * PAIR + i
                            totals[s] = (
                                totals[s]
                                + sa[p, row : row + 1, :] * straight
                                + sb[p, row : row + 1, :] * turned
                            )
            for s in range(SHOTS):
                pred[p, s, k] = totals[s]
            return 0

        lax.fori_loop(0, PIECES, piece, 0)
        each(PIECES, lambda j: fifth(k, j, to_p).start())
        for s in range(SHOTS):
            bands[f, s, mine, k] = pred[mine, s, k]

    def choose(k):
        own_piece(k).wait()
        each(PIECES, lambda j: first(k, j, here).wait_recv())
        for b in range(STEPS):
            total = jnp.zeros((POINTS_BLK, SUB, LANES), F32)
            for p in range(PIECES):
                total = total + weights[b, p] * r1[k, p]
            m[k, b] = total
        each(NZ, lambda j: second(k, j, to_z).start())
        for b in range(STEPS):
            r2[k, z, b] = m[k, b, pl.ds(z * PAIR, PAIR)]

    def gather(k):
        each(PIECES, lambda j: fifth(k, j, here).wait_recv())
        each(NQ, lambda j: sixth(k, j, to_f).start())

    def across(k):
        each(NZ, lambda j: second(k, j, here).wait_recv())
        for b in range(STEPS):
            total = jnp.zeros((PAIR, SUB, LANES), F32)
            for o in range(NZ):
                total = total + weights[b, PIECES + o] * r2[k, o, b]
            hown[k, b] = total
        third(k).start()

    def share(k):
        third(k).wait_recv()
        for b in range(STEPS):
            ag[k, z, b] = (
                weights[b, PIECES + NZ] * hown[k, b] + weights[b, PIECES + NZ + 1] * hin[k, b]
            )
        each(NZ, lambda j: fourth(k, j, to_z).start())

    def tick(t, _):
        @pl.when(t >= 1)
        def _():
            predict(t - 1)

        @pl.when(t < CHUNKS)
        def _():
            choose(t)

        @pl.when(t >= 1)
        def _():
            gather(t - 1)

        @pl.when(t < CHUNKS)
        def _():
            across(t)
            share(t)

        return 0

    lax.fori_loop(0, CHUNKS + 1, tick, 0)

    filt_h(1 - h).wait_recv()

    def finish(k, _):
        each(NQ, lambda j: sixth(k, j, here).wait_recv())
        each(PIECES, lambda j: first(k, j, to_p).wait_send())
        each(NZ, lambda j: second(k, j, to_z).wait_send())
        third(k).wait_send()
        each(NZ, lambda j: fourth(k, j, to_z).wait_send())
        each(PIECES, lambda j: fifth(k, j, to_p).wait_send())
        each(NQ, lambda j: sixth(k, j, to_f).wait_send())
        return 0

    lax.fori_loop(0, CHUNKS, finish, 0)
    each(NQ, lambda j: spec_f(j, to_f).wait_send())
    each(PIECES, lambda j: spec_p(j, to_p).wait_send())
    each(PIECES, lambda j: filt_p(j, to_p).wait_send())
    each(NZ, lambda j: filt_z(j, to_z).wait_send())
    filt_h(h).wait_send()


def spread(traces, live, cols, wave, surface, weights, filt):
    dma = pltpu.SemaphoreType.DMA
    v = pltpu.VMEM
    tile = (SUB, LANES)
    vm = pl.BlockSpec(memory_space=pltpu.VMEM)
    small = (STEPS, PAIR, *tile)
    return pl.pallas_call(
        spread_kernel,
        out_shape=(
            jax.ShapeDtypeStruct((NQ, SHOTS, PIECES, CHUNKS, *tile), F32),
            jax.ShapeDtypeStruct((NH, NZ, PIECES, 128), F32),
        ),
        in_specs=[
            vm, vm, vm, vm,
            pl.BlockSpec(memory_space=pl.ANY),
            pl.BlockSpec(memory_space=pltpu.SMEM),
            vm,
        ],
        out_specs=(vm, vm),
        scratch_shapes=[
            v((CHUNKS, PIECES, POINTS_BLK, *tile), F32),
            v((CHUNKS, STEPS, POINTS_BLK, *tile), F32),
            v((CHUNKS, NZ, *small), F32),
            v((CHUNKS, *small), F32),
            v((CHUNKS, *small), F32),
            v((CHUNKS, NZ, *small), F32),
            v((NQ, SHOTS * COLS, LANES), F32),
            v((NQ, SHOTS * COLS, LANES), F32),
            v((PIECES, SHOTS * COLS, LANES), F32),
            v((PIECES, SHOTS * COLS, LANES), F32),
            v((PIECES, SHOTS * COLS, LANES), F32),
            v((NZ, *small), F32),
            v((PIECES, SHOTS, CHUNKS, *tile), F32),
            v((PIECES, 8, 128), F32),
            v((PIECES, 128), F32),
            dma((CHUNKS, PIECES)), dma((CHUNKS, PIECES)),
            dma((CHUNKS, NZ)), dma((CHUNKS, NZ)),
            dma((CHUNKS,)), dma((CHUNKS,)),
            dma((CHUNKS, NZ)), dma((CHUNKS, NZ)),
            dma((CHUNKS, PIECES)), dma((CHUNKS, PIECES)),
            dma((CHUNKS, NQ)), dma((CHUNKS, NQ)),
            dma((NQ,)), dma((NQ,)),
            dma((PIECES,)), dma((PIECES,)),
            dma((PIECES,)), dma((PIECES,)),
            dma((NZ,)), dma((NZ,)),
            dma, dma,
            dma((CHUNKS,)),
        ],
        compiler_params=pltpu.CompilerParams(
            collective_id=0, has_side_effects=True, vmem_limit_bytes=40 * 2**20
        ),
    )(traces, live, cols, wave, surface, weights, filt)


TILE = 192


def clean_kernel(
    bands, table, rowids, live, traces, slots, edge, combine, taps, out, cleaned
):
    def rows(i, _):
        at = pl.ds(pl.multiple_of(i * TILE, TILE), TILE)
        lane = lax.broadcasted_iota(jnp.int32, (TILE, 128), 1)
        ids = rowids[at, :]
        pick = jnp.where(lane == ids[:, 0:1], 1.0, 0.0)
        four = jnp.dot(pick, table[...], precision=FULL, preferred_element_type=F32)
        low = ids[:, 1:2]
        four = jnp.where((lane >= low) & (lane < low + TAPS), four, 0.0)
        factor = jnp.dot(four, taps[...], precision=FULL, preferred_element_type=F32)
        blocks = [bands[o, at, :] for o in range(NQ)]
        ends = jnp.zeros((TILE, 128), F32)
        for o in range(NQ):
            ends = ends + jnp.dot(
                blocks[o], edge[o * LANES : (o + 1) * LANES, :],
                precision=FULL, preferred_element_type=F32,
            )
        blocks.append(ends)
        total = jnp.zeros((TILE, QUARTER), F32)
        width = (NQ + 1) * LANES
        for o in range(NQ + 1):
            span = slice(o * LANES, (o + 1) * LANES)
            cross = slice(width + o * LANES, width + (o + 1) * LANES)
            mixed = blocks[o] * factor[:, span]
            mixed = mixed + pltpu.roll(blocks[o], BAND, 1) * factor[:, cross]
            total = total + jnp.dot(
                mixed, combine[span, :], precision=FULL, preferred_element_type=F32
            )
        cleaned[at, :] = live[at, :] * (traces[at, :] - total)
        return 0

    lax.fori_loop(0, ROWS // TILE, rows, 0)

    def place_rows(i, _):
        ids = lax.broadcasted_iota(jnp.int32, (128, ROWS), 0) + i * 128
        pick = jnp.where(ids == slots[...], 1.0, 0.0)
        out[pl.ds(pl.multiple_of(i * 128, 128), 128), :] = jnp.dot(
            pick, cleaned[...], precision=FULL, preferred_element_type=F32
        )
        return 0

    lax.fori_loop(0, out.shape[0] // 128, place_rows, 0)


def clean(*args):
    vm = pl.BlockSpec(memory_space=pltpu.VMEM)
    return pl.pallas_call(
        clean_kernel,
        out_shape=jax.ShapeDtypeStruct((1024, QUARTER), F32),
        in_specs=[vm] * len(args),
        out_specs=vm,
        scratch_shapes=[pltpu.VMEM((ROWS, QUARTER), F32)],
        compiler_params=pltpu.CompilerParams(vmem_limit_bytes=40 * 2**20),
    )(*args)


def on_device(traces, live_mask, offset_bin, surface, block_owner, point_column, filters):
    x, z, h, c, f = place()
    live = live_mask.astype(F32)
    owner = block_owner[:, None]
    piece = owner // (NZ * NH * NC) * NC + owner % NC
    same_h = owner // NC % NH == h
    weights = jnp.concatenate(
        [
            piece == jnp.arange(PIECES)[None, :],
            owner // (NH * NC) % NZ == jnp.arange(NZ)[None, :],
            same_h,
            ~same_h,
        ],
        axis=1,
    ).astype(F32)
    filt = jnp.pad(filters.reshape(1, 4 * TAPS), ((0, 7), (0, 128 - 4 * TAPS)))
    wave = lax.dynamic_index_in_dim(jnp.asarray(FORWARD), f, 0, keepdims=False)
    edge = lax.dynamic_index_in_dim(jnp.asarray(EDGE_IN), f, 0, keepdims=False)
    combine = lax.dynamic_index_in_dim(jnp.asarray(COMBINE), f, 0, keepdims=False)
    bands, table = spread(
        traces, live, point_column.reshape(COLS, 1), wave, surface, weights, filt
    )
    bins = offset_bin.reshape(ROWS)
    order = jnp.arange(ROWS)
    earlier = (bins[:, None] == bins[None, :]) & (order[None, :] < order[:, None])
    slots = bins * 2 + jnp.sum(earlier.astype(jnp.int32), axis=1)
    home = bins // 4
    row = home // NC % NH * (NZ * PIECES) + home // (NH * NC) % NZ * PIECES
    row = row + home // (NZ * NH * NC) * NC + home % NC
    rowids = jnp.stack([row, bins % 4 * TAPS], axis=1)
    packed = clean(
        bands.reshape(NQ, ROWS, LANES),
        table.reshape(128, 128),
        rowids,
        live.reshape(ROWS, 1),
        traces.reshape(ROWS, QUARTER),
        slots.reshape(1, ROWS),
        edge,
        combine,
        jnp.asarray(TAP_TABLE),
    )
    packed = packed.reshape(128, 8, QUARTER)
    dealt = lax.all_to_all(packed, "shot", split_axis=0, concat_axis=0, tiled=True)
    dealt = dealt.reshape(128, 4, 2, QUARTER).transpose(1, 0, 2, 3)
    return dealt.reshape(4, 256, QUARTER)


def solution(mesh):
    return jax.shard_map(
        on_device,
        mesh=mesh,
        in_specs=(
            P("shot", None, "freq"),
            P("shot", None),
            P("shot", None, None),
            P("shot", None, "freq"),
            P(),
            P(),
            P("shot", None),
        ),
        out_specs=P("shot", None, "freq"),
        check_vma=False,
    )
```

time: 1990 us -> 217 us (0.11)
  the two profiles are of different devices: /device:TPU:1 before, /device:TPU:16 now
where the time goes in v1:
time: 217 us; the launch traced here: 216 us
  Pallas kernels  159 us (73%)
  blocking collectives  44.1 us (20%)
  local copies, waits for them, and re-layouts  9 us (4%)
  other arithmetic  4.06 us (2%)
    pallas_call x1, Pallas kernels, spread(): pl.pallas_call(spread_kernel, out_shape=(jax.ShapeDtypeStruct((NQ, SHOTS,...  142 us
    all_to_all x1, blocking collectives, on_device(): lax.all_to_all(packed, 'shot', split_axis=0, concat_axis=0, tiled=True)  44.1 us
    pallas_call x1, Pallas kernels, clean(): pl.pallas_call(clean_kernel, out_shape=jax.ShapeDtypeStruct((1024, QUARTE...  17.5 us

profile of v1, /device:TPU:16, one launch (start us, length us, event | category | flops | bytes accessed | tf_op | source)
XLA Modules:
  0.0 216.4 jit_solution(10145335372072566442)
XLA Ops:
  0.0 0.0 copy-start
  0.0 0.0 copy-start.1
  0.0 0.9 reshape.442
  0.9 0.7 fusion.9
  1.6 0.7 compare_bitcast_fusion
  2.3 0.1 copy.31
  2.4 0.1 copy.32
  2.5 0.7 fusion.12
  3.2 0.8 fusion.1
  4.0 0.4 convert_reduce_fusion
  4.4 0.7 convert_bitcast_fusion
  5.1 0.8 reshape.451.cols
  5.8 0.2 copy.34.rowids
  6.0 0.9 copy.38
  7.0 1.0 dynamic-slice_bitcast_fusion.2.edge
  8.0 1.1 dynamic-slice_bitcast_fusion.1.wave
  9.0 0.0 copy-start.2
  9.1 0.0 copy-start.3
  9.1 1.2 dynamic-slice_bitcast_fusion.combine
  10.3 0.1 iota_compare_fusion.1
  10.4 0.1 add_convert_fusion.weights
  10.5 0.0 copy-done
  10.5 0.0 copy-done.1
  10.5 141.6 %shard_map.109 = (f32[4,3,8,4,8,128]{5,4,3,2,1,0:T(8,128)S(1)}, f32[2,8,8,128]{3,2,1,0:T(8,128)S(1)}) custom-call(f32[3,256,256]{2,1,0:T(8,128)S(1)} %copy-done, f32[3,256]{1,0:T(4,128)S(1)} %get-tuple-element.14.live, s32[32,1]{1,0:T(8,128)S(1)} %reshape.451.cols, f32[256,512]{1,0:T(8,128)S(1)} %dynamic-slice_bitcast_fusion.1.wave, ...), custom_call_target="tpu_custom_call" | custom-call | tf_op jit(solution)/shard_map/pallas_call | solution.py:357
  152.1 0.0 copy-done.2
  152.1 0.0 copy-done.3
  152.1 17.5 %shard_map.110 = f32[1024,256]{1,0:T(8,128)S(1)} custom-call(f32[4,768,128]{2,1,0:T(8,128)S(1)} %bitcast.27, f32[128,128]{1,0:T(8,128)S(1)} %bitcast.28, s32[768,2]{1,0:T(8,128)S(1)} %copy.34.rowids, f32[768,1]{1,0:T(8,128)S(1)} %bitcast.26, f32[768,256]{1,0:T(8,128)S(1)} %bitcast.25, s32[1,768]{1,0:T(1,128)S(1)} %reshape_add_fusion.slots, ...), custom_call_target="tpu_custom_call" | custom-call | tf_op jit(solution)/shard_map/pallas_call | solution.py:456
  169.6 44.1 %all_to_all.5 = f32[128,8,256]{2,1,0:T(8,128)S(1)} all-to-all(f32[128,8,256]{2,1,0:T(8,128)S(1)} %bitcast.24), channel_id=1, replica_groups=mesh['shot'=128,'freq'=4] {'shot'}, dimensions={0} | all-to-all | bytes 2097152 | tf_op jit(solution)/shard_map/all_to_all | solution.py:508
  213.7 0.6 reshape.449
  214.3 0.4 copy.40
  214.7 1.7 reshape.450
  (7 shorter events, 0.1 us)
Async XLA Ops:
  0.0 10.5 %copy-start = (f32[3,256,256]{2,1,0:T(8,128)S(1)}, f32[3,256,256]{2,1,0:T(8,128)}, u32[]{:S(2)}) copy-start(f32[3,256,256]{2,1,0:T(8,128)} %traces.1) | copy-start | bytes 2359300
  0.0 10.5 %copy-start.1 = (f32[16,256,128]{2,1,0:T(8,128)S(1)}, f32[16,256,128]{2,1,0:T(8,128)}, u32[]{:S(2)}) copy-start(f32[16,256,128]{2,1,0:T(8,128)} %surface.1) | copy-start | bytes 6291460
  9.0 143.1 %copy-start.2 = (f32[1,768]{0,1:T(8,128)S(1)}, f32[1,768]{0,1:T(8,128)}, u32[]{:S(2)}) copy-start(f32[1,768]{0,1:T(8,128)} %copy.38) | copy-start | bytes 9220
  9.1 143.1 %copy-start.3 = (f32[128,1280]{1,0:T(8,128)S(1)}, f32[128,1280]{1,0:T(8,128)}, u32[]{:S(2)}) copy-start(f32[128,1280]{1,0:T(8,128)} %constant.176.clone.taps) | copy-start | bytes 1966084

commit v2 on v1

--- a/solution.py
+++ b/solution.py
@@ -1,8 +1,6 @@
-import functools
-import math
-
 import jax
 import jax.numpy as jnp
+import ml_dtypes
 import numpy as np
 from jax import lax
 from jax.experimental import pallas as pl
@@ -31,6 +29,8 @@
 FULL = lax.Precision.HIGHEST
 MESH = pl.DeviceIdType.MESH
 F32 = jnp.float32
+B16 = jnp.bfloat16
+I32 = jnp.int32
 
 
 def tables():
@@ -70,10 +70,33 @@
     cross2 = np.concatenate([np.sin(lag2), -np.sin(lag2)], axis=1)
     taps = np.concatenate([same, same2, cross, cross2], axis=1)
     taps = np.concatenate([taps] * 4 + [np.zeros((4, taps.shape[1]))], axis=0)
-    return [np.asarray(a, np.float32) for a in (forward, edge, combine, taps)]
+    return forward, edge, combine, taps
+
+
+def halves(a):
+    top = a.astype(ml_dtypes.bfloat16)
+    return top, (a - top.astype(np.float64)).astype(ml_dtypes.bfloat16)
 
 
 FORWARD, EDGE_IN, COMBINE, TAP_TABLE = tables()
+FORWARD = FORWARD.astype(np.float32)
+EDGE_HI, EDGE_LO = halves(EDGE_IN)
+COMBINE_HI, COMBINE_LO = halves(COMBINE)
+TAP_HI, TAP_LO = halves(TAP_TABLE)
+
+
+def dot(a, b):
+    return jnp.dot(a, b, preferred_element_type=F32)
+
+
+def split(a):
+    top = a.astype(B16)
+    return top, (a - top.astype(F32)).astype(B16)
+
+
+def dot3(a, top, low):
+    a_top, a_low = split(a)
+    return dot(a_top, top) + (dot(a_low, top) + dot(a_top, low))
 
 
 def place():
@@ -87,10 +110,14 @@
 
 
 def spread_kernel(
-    traces, live, cols, wave, surface, weights, filt, bands, table,
+    traces, live, bins, cols, owner, surface, filters,
+    wave_all, edge_hi_all, edge_lo_all, combine_hi_all, combine_lo_all, tap_hi, tap_lo,
+    packed,
+    bands, table, wave, edge_hi, edge_lo, combine_hi, combine_lo,
+    onehot, factor, cleaned, clean_hi, clean_lo, slots, rows8, bin_col, live_col, filt, f1x,
     r1, m, r2, hown, hin, ag, specp, specr, specall, sa, sb, srot, pred, f1, f1c,
     s1s, s1r, s2s, s2r, hs, hr, gs, gr, bs, br, fs, fr,
-    ps, pr, cs, cr, u1s, u1r, u2s, u2r, us, ur, own,
+    ps, pr, cs, cr, u1s, u1r, u2s, u2r, us, ur, own, consts,
 ):
     x, z, h, c, f = place()
     mine = x * NC + c
@@ -194,6 +221,8 @@
     def here(o):
         return o
 
+    filt[...] = jnp.zeros((SUB, 128), F32)
+    filt[0:4, 0:TAPS] = filters[...]
     each(PIECES, lambda j: filt_p(j, to_p).start())
 
     def start_first(k, _):
@@ -209,20 +238,59 @@
     for k in range(CHUNKS):
         own_piece(k).start()
 
-    at_point = lax.broadcasted_iota(jnp.int32, (COLS, R), 1) == cols[...]
+    held = [
+        pltpu.make_async_copy(whole.at[f], part, consts.at[i])
+        for i, (whole, part) in enumerate((
+            (wave_all, wave), (edge_hi_all, edge_hi), (edge_lo_all, edge_lo),
+            (combine_hi_all, combine_hi), (combine_lo_all, combine_lo),
+        ))
+    ]
+    for one in held:
+        one.start()
+
+    weights = []
+    for b in range(STEPS):
+        who = owner[b]
+        who_p = (who >> 5) * NC + (who & 1)
+        who_z = (who >> 2) & (NZ - 1)
+        who_h = (who >> 1) & 1
+        weights.append(
+            [jnp.where(who_p == p, 1.0, 0.0) for p in range(PIECES)]
+            + [jnp.where(who_z == o, 1.0, 0.0) for o in range(NZ)]
+            + [jnp.where(who_h == h, 1.0, 0.0), jnp.where(who_h == h, 0.0, 1.0)]
+        )
+
+    lane_row = lax.broadcasted_iota(I32, (1, R), 1)
+    for b in range(STEPS):
+        for j in range(POINTS_BLK):
+            row = b * POINTS_BLK + j
+            onehot[row : row + 1, :] = jnp.where(lane_row == cols[b, j], 1.0, 0.0)
+    held[0].wait()
+    picked = []
     for s in range(SHOTS):
-        pick = jnp.where(at_point, live[s : s + 1, :], 0.0)
-        picked = jnp.dot(pick, traces[s], precision=FULL, preferred_element_type=F32)
-        part = jnp.dot(picked, wave[...], precision=FULL, preferred_element_type=F32)
-        for o in range(NQ):
-            specp[o, s * COLS : (s + 1) * COLS, :] = part[:, o * LANES : (o + 1) * LANES]
+        pick = onehot[...] * live[s : s + 1, :].astype(F32)
+        picked.append(
+            jnp.dot(
+                pick, traces[s].reshape(R, QUARTER), precision=FULL, preferred_element_type=F32
+            )
+        )
+    part = jnp.dot(
+        jnp.concatenate(picked, axis=0), wave[...], precision=FULL, preferred_element_type=F32
+    )
+    for o in range(NQ):
+        specp[o] = part[:, o * LANES : (o + 1) * LANES]
     each(NQ, lambda j: spec_f(j, to_f).start())
     specr[f] = specp[f]
 
     f1[mine] = filt[...]
     each(PIECES, lambda j: filt_p(j, here).wait_recv())
     for p in range(PIECES):
-        f1c[p : p + 1, :] = f1[p, 0:1, :]
+        for i in range(4):
+            f1x[i, p : p + 1, :] = f1[p, i : i + 1, :]
+    lined = f1x[0]
+    for i in range(1, 4):
+        lined = lined + pltpu.roll(f1x[i], i * TAPS, 1)
+    f1c[...] = lined
     each(NZ, lambda j: filt_z(j, to_z).start())
 
     each(NQ, lambda j: spec_f(j, here).wait_recv())
@@ -232,6 +300,26 @@
     table[h, z] = f1c[...]
     each(NZ, lambda j: filt_z(j, here).wait_recv())
     filt_h(h).start()
+
+    rows8[...] = jnp.zeros((SUB, R), I32)
+    rows8[0:SHOTS, :] = bins[...]
+    rows8[SHOTS : 2 * SHOTS, :] = live[...]
+    turned_rows = rows8[...].T
+    for s in range(SHOTS):
+        bin_col[s] = turned_rows[:, s : s + 1].reshape(PIECES, CHUNKS, SUB, 1)
+        live_col[s] = turned_rows[:, SHOTS + s : SHOTS + s + 1].reshape(PIECES, CHUNKS, SUB, 1)
+    for s in range(SHOTS):
+        row = bins[s : s + 1, :]
+        count = jnp.zeros((1, R), I32)
+        for o in range(s + 1):
+            hit = jnp.where(turned_rows[:, o : o + 1] == row, 1, 0)
+            if o == s:
+                before = lax.broadcasted_iota(I32, (R, R), 0) < lax.broadcasted_iota(
+                    I32, (R, R), 1
+                )
+                hit = jnp.where(before, hit, 0)
+            count = count + jnp.sum(hit, axis=0, keepdims=True)
+        slots[:, s * R : (s + 1) * R] = row * 2 + count
 
     each(PIECES, lambda j: spec_p(j, here).wait_recv())
     low = lax.broadcasted_iota(jnp.int32, (SHOTS * COLS, LANES), 1) < BAND
@@ -279,7 +367,7 @@
         for b in range(STEPS):
             total = jnp.zeros((POINTS_BLK, SUB, LANES), F32)
             for p in range(PIECES):
-                total = total + weights[b, p] * r1[k, p]
+                total = total + weights[b][p] * r1[k, p]
             m[k, b] = total
         each(NZ, lambda j: second(k, j, to_z).start())
         for b in range(STEPS):
@@ -294,7 +382,7 @@
         for b in range(STEPS):
             total = jnp.zeros((PAIR, SUB, LANES), F32)
             for o in range(NZ):
-                total = total + weights[b, PIECES + o] * r2[k, o, b]
+                total = total + weights[b][PIECES + o] * r2[k, o, b]
             hown[k, b] = total
         third(k).start()
 
@@ -302,36 +390,83 @@
         third(k).wait_recv()
         for b in range(STEPS):
             ag[k, z, b] = (
-                weights[b, PIECES + NZ] * hown[k, b] + weights[b, PIECES + NZ + 1] * hin[k, b]
+                weights[b][PIECES + NZ] * hown[k, b] + weights[b][PIECES + NZ + 1] * hin[k, b]
             )
         each(NZ, lambda j: fourth(k, j, to_z).start())
 
+    tile = SHOTS * PIECES * SUB
+
+    def prepare(k):
+        lane = lax.broadcasted_iota(I32, (tile, 128), 1)
+        one = bin_col[:, :, k].reshape(tile, 1)
+        home = one >> 2
+        line = ((home >> 1) & 1) * (NZ * PIECES) + ((home >> 2) & (NZ - 1)) * PIECES
+        line = line + (home >> 5) * NC + (home & 1)
+        pick = jnp.where(lane == line, 1.0, 0.0).astype(B16)
+        all_taps = table[...].reshape(128, 128)
+        top, rest = split(all_taps)
+        middle, last = split(all_taps - top.astype(F32))
+        four = dot(pick, top) + (dot(pick, middle) + dot(pick, last))
+        start = (one & 3) * TAPS
+        four = jnp.where((lane >= start) & (lane < start + TAPS), four, 0.0)
+        factor[k] = dot3(four, tap_hi[...], tap_lo[...])
+
+    def clean(k):
+        each(NQ, lambda j: sixth(k, j, here).wait_recv())
+        blocks = [bands[o, :, :, k].reshape(tile, LANES) for o in range(NQ)]
+        ends = jnp.zeros((tile, 128), F32)
+        for o in range(NQ):
+            span = slice(o * LANES, (o + 1) * LANES)
+            ends = ends + dot3(blocks[o], edge_hi[span, :], edge_lo[span, :])
+        blocks.append(ends)
+        total = jnp.zeros((tile, QUARTER), F32)
+        width = (NQ + 1) * LANES
+        for o in range(NQ + 1):
+            span = slice(o * LANES, (o + 1) * LANES)
+            cross = slice(width + o * LANES, width + (o + 1) * LANES)
+            mixed = blocks[o] * factor[k, :, span]
+            mixed = mixed + pltpu.roll(blocks[o], BAND, 1) * factor[k, :, cross]
+            total = total + dot3(mixed, combine_hi[span, :], combine_lo[span, :])
+        alive = live_col[:, :, k].reshape(tile, 1).astype(F32)
+        whole = traces[:, :, k].reshape(tile, QUARTER)
+        cleaned[:, :, k] = (alive * (whole - total)).reshape(SHOTS, PIECES, SUB, QUARTER)
+
+    def stage(t, lag, fn):
+        @pl.when((t >= lag) & (t < lag + CHUNKS))
+        def _():
+            fn(t - lag)
+
+    for one in held[1:]:
+        one.wait()
+    filt_h(1 - h).wait_recv()
+
     def tick(t, _):
-        @pl.when(t >= 1)
-        def _():
-            predict(t - 1)
-
-        @pl.when(t < CHUNKS)
-        def _():
-            choose(t)
-
-        @pl.when(t >= 1)
-        def _():
-            gather(t - 1)
-
-        @pl.when(t < CHUNKS)
-        def _():
-            across(t)
-            share(t)
-
+        stage(t, 5, clean)
+        stage(t, 4, gather)
+        stage(t, 3, predict)
+        stage(t, 2, share)
+        stage(t, 1, across)
+        stage(t, 1, prepare)
+        stage(t, 0, choose)
         return 0
 
-    lax.fori_loop(0, CHUNKS + 1, tick, 0)
-
-    filt_h(1 - h).wait_recv()
+    lax.fori_loop(0, CHUNKS + 5, tick, 0)
+
+    top, rest = split(cleaned[...].reshape(ROWS, QUARTER))
+    clean_hi[...] = top
+    clean_lo[...] = rest
+
+    def place_rows(i, _):
+        ids = lax.broadcasted_iota(I32, (128, ROWS), 0) + i * 128
+        pick = jnp.where(ids == slots[...], 1.0, 0.0).astype(B16)
+        packed[pl.ds(pl.multiple_of(i * 128, 128), 128), :] = dot(pick, clean_hi[...]) + dot(
+            pick, clean_lo[...]
+        )
+        return 0
+
+    lax.fori_loop(0, packed.shape[0] // 128, place_rows, 0)
 
     def finish(k, _):
-        each(NQ, lambda j: sixth(k, j, here).wait_recv())
         each(PIECES, lambda j: first(k, j, to_p).wait_send())
         each(NZ, lambda j: second(k, j, to_z).wait_send())
         third(k).wait_send()
@@ -348,26 +483,36 @@
     filt_h(h).wait_send()
 
 
-def spread(traces, live, cols, wave, surface, weights, filt):
+def spread(*args):
     dma = pltpu.SemaphoreType.DMA
     v = pltpu.VMEM
     tile = (SUB, LANES)
     vm = pl.BlockSpec(memory_space=pltpu.VMEM)
+    sm = pl.BlockSpec(memory_space=pltpu.SMEM)
+    hbm = pl.BlockSpec(memory_space=pltpu.HBM)
     small = (STEPS, PAIR, *tile)
+    wide = (NQ + 1) * LANES
     return pl.pallas_call(
         spread_kernel,
-        out_shape=(
-            jax.ShapeDtypeStruct((NQ, SHOTS, PIECES, CHUNKS, *tile), F32),
-            jax.ShapeDtypeStruct((NH, NZ, PIECES, 128), F32),
-        ),
-        in_specs=[
-            vm, vm, vm, vm,
-            pl.BlockSpec(memory_space=pl.ANY),
-            pl.BlockSpec(memory_space=pltpu.SMEM),
-            vm,
-        ],
-        out_specs=(vm, vm),
+        out_shape=jax.ShapeDtypeStruct((1024, QUARTER), F32),
+        in_specs=[vm, vm, vm, sm, sm, hbm, vm, hbm, hbm, hbm, hbm, hbm, vm, vm],
+        out_specs=vm,
         scratch_shapes=[
+            v((NQ, SHOTS, PIECES, CHUNKS, *tile), F32),
+            v((NH, NZ, PIECES, 128), F32),
+            v((QUARTER, NQ * LANES), F32),
+            v((NQ * LANES, 128), B16), v((NQ * LANES, 128), B16),
+            v((wide, QUARTER), B16), v((wide, QUARTER), B16),
+            v((COLS, R), F32),
+            v((CHUNKS, SHOTS * PIECES * SUB, 2 * wide), F32),
+            v((SHOTS, PIECES, CHUNKS, SUB, QUARTER), F32),
+            v((ROWS, QUARTER), B16), v((ROWS, QUARTER), B16),
+            v((1, ROWS), I32),
+            v((SUB, R), I32),
+            v((SHOTS, PIECES, CHUNKS, SUB, 1), I32),
+            v((SHOTS, PIECES, CHUNKS, SUB, 1), I32),
+            v((SUB, 128), F32),
+            v((4, PIECES, 128), F32),
             v((CHUNKS, PIECES, POINTS_BLK, *tile), F32),
             v((CHUNKS, STEPS, POINTS_BLK, *tile), F32),
             v((CHUNKS, NZ, *small), F32),
@@ -395,114 +540,26 @@
             dma((NZ,)), dma((NZ,)),
             dma, dma,
             dma((CHUNKS,)),
+            dma((5,)),
         ],
         compiler_params=pltpu.CompilerParams(
-            collective_id=0, has_side_effects=True, vmem_limit_bytes=40 * 2**20
+            collective_id=0, has_side_effects=True, vmem_limit_bytes=48 * 2**20
         ),
-    )(traces, live, cols, wave, surface, weights, filt)
-
-
-TILE = 192
-
-
-def clean_kernel(
-    bands, table, rowids, live, traces, slots, edge, combine, taps, out, cleaned
-):
-    def rows(i, _):
-        at = pl.ds(pl.multiple_of(i * TILE, TILE), TILE)
-        lane = lax.broadcasted_iota(jnp.int32, (TILE, 128), 1)
-        ids = rowids[at, :]
-        pick = jnp.where(lane == ids[:, 0:1], 1.0, 0.0)
-        four = jnp.dot(pick, table[...], precision=FULL, preferred_element_type=F32)
-        low = ids[:, 1:2]
-        four = jnp.where((lane >= low) & (lane < low + TAPS), four, 0.0)
-        factor = jnp.dot(four, taps[...], precision=FULL, preferred_element_type=F32)
-        blocks = [bands[o, at, :] for o in range(NQ)]
-        ends = jnp.zeros((TILE, 128), F32)
-        for o in range(NQ):
-            ends = ends + jnp.dot(
-                blocks[o], edge[o * LANES : (o + 1) * LANES, :],
-                precision=FULL, preferred_element_type=F32,
-            )
-        blocks.append(ends)
-        total = jnp.zeros((TILE, QUARTER), F32)
-        width = (NQ + 1) * LANES
-        for o in range(NQ + 1):
-            span = slice(o * LANES, (o + 1) * LANES)
-            cross = slice(width + o * LANES, width + (o + 1) * LANES)
-            mixed = blocks[o] * factor[:, span]
-            mixed = mixed + pltpu.roll(blocks[o], BAND, 1) * factor[:, cross]
-            total = total + jnp.dot(
-                mixed, combine[span, :], precision=FULL, preferred_element_type=F32
-            )
-        cleaned[at, :] = live[at, :] * (traces[at, :] - total)
-        return 0
-
-    lax.fori_loop(0, ROWS // TILE, rows, 0)
-
-    def place_rows(i, _):
-        ids = lax.broadcasted_iota(jnp.int32, (128, ROWS), 0) + i * 128
-        pick = jnp.where(ids == slots[...], 1.0, 0.0)
-        out[pl.ds(pl.multiple_of(i * 128, 128), 128), :] = jnp.dot(
-            pick, cleaned[...], precision=FULL, preferred_element_type=F32
-        )
-        return 0
-
-    lax.fori_loop(0, out.shape[0] // 128, place_rows, 0)
-
-
-def clean(*args):
-    vm = pl.BlockSpec(memory_space=pltpu.VMEM)
-    return pl.pallas_call(
-        clean_kernel,
-        out_shape=jax.ShapeDtypeStruct((1024, QUARTER), F32),
-        in_specs=[vm] * len(args),
-        out_specs=vm,
-        scratch_shapes=[pltpu.VMEM((ROWS, QUARTER), F32)],
-        compiler_params=pltpu.CompilerParams(vmem_limit_bytes=40 * 2**20),
     )(*args)
 
 
 def on_device(traces, live_mask, offset_bin, surface, block_owner, point_column, filters):
-    x, z, h, c, f = place()
-    live = live_mask.astype(F32)
-    owner = block_owner[:, None]
-    piece = owner // (NZ * NH * NC) * NC + owner % NC
-    same_h = owner // NC % NH == h
-    weights = jnp.concatenate(
-        [
-            piece == jnp.arange(PIECES)[None, :],
-            owner // (NH * NC) % NZ == jnp.arange(NZ)[None, :],
-            same_h,
-            ~same_h,
-        ],
-        axis=1,
-    ).astype(F32)
-    filt = jnp.pad(filters.reshape(1, 4 * TAPS), ((0, 7), (0, 128 - 4 * TAPS)))
-    wave = lax.dynamic_index_in_dim(jnp.asarray(FORWARD), f, 0, keepdims=False)
-    edge = lax.dynamic_index_in_dim(jnp.asarray(EDGE_IN), f, 0, keepdims=False)
-    combine = lax.dynamic_index_in_dim(jnp.asarray(COMBINE), f, 0, keepdims=False)
-    bands, table = spread(
-        traces, live, point_column.reshape(COLS, 1), wave, surface, weights, filt
-    )
-    bins = offset_bin.reshape(ROWS)
-    order = jnp.arange(ROWS)
-    earlier = (bins[:, None] == bins[None, :]) & (order[None, :] < order[:, None])
-    slots = bins * 2 + jnp.sum(earlier.astype(jnp.int32), axis=1)
-    home = bins // 4
-    row = home // NC % NH * (NZ * PIECES) + home // (NH * NC) % NZ * PIECES
-    row = row + home // (NZ * NH * NC) * NC + home % NC
-    rowids = jnp.stack([row, bins % 4 * TAPS], axis=1)
-    packed = clean(
-        bands.reshape(NQ, ROWS, LANES),
-        table.reshape(128, 128),
-        rowids,
-        live.reshape(ROWS, 1),
-        traces.reshape(ROWS, QUARTER),
-        slots.reshape(1, ROWS),
-        edge,
-        combine,
-        jnp.asarray(TAP_TABLE),
+    packed = spread(
+        traces.reshape(SHOTS, PIECES, CHUNKS, SUB, QUARTER),
+        live_mask,
+        offset_bin.reshape(SHOTS, R),
+        point_column,
+        block_owner,
+        surface,
+        filters,
+        *(jnp.asarray(a) for a in (FORWARD, EDGE_HI, EDGE_LO, COMBINE_HI, COMBINE_LO)),
+        jnp.asarray(TAP_HI),
+        jnp.asarray(TAP_LO),
     )
     packed = packed.reshape(128, 8, QUARTER)
     dealt = lax.all_to_all(packed, "shot", split_axis=0, concat_axis=0, tiled=True)

time: 217 us -> 175 us (0.81)
  the two profiles are of different devices: /device:TPU:16 before, /device:TPU:9 now
where the time goes in v2:
time: 175 us
  Pallas kernels  111 us (63%)
  blocking collectives  49.8 us (28%)
  local copies, waits for them, and re-layouts  13.8 us (8%)
    pallas_call x1, Pallas kernels, spread(): pl.pallas_call(spread_kernel, out_shape=jax.ShapeDtypeStruct((1024, QUART...  111 us
    all_to_all x1, blocking collectives, on_device(): lax.all_to_all(packed, 'shot', split_axis=0, concat_axis=0, tiled=True)  49.8 us
    unnamed x23, local copies, waits for them, and re-layouts  11.2 us

profile of v2, /device:TPU:9, one launch (start us, length us, event | category | flops | bytes accessed | tf_op | source)
XLA Modules:
  0.0 174.9 jit_solution(3009967781535092408)
XLA Ops:
  0.0 0.7 copy.20
  0.7 0.0 copy-start
  0.7 1.3 copy-done
  2.0 0.0 copy-start.1
  2.0 1.3 copy-done.1
  3.3 0.0 copy-start.2
  3.3 1.1 copy-done.2
  4.5 0.0 copy-start.3
  4.5 1.0 copy-done.3
  5.5 0.0 copy-start.4
  5.5 1.0 copy-done.4
  6.5 0.0 copy-start.5
  6.5 1.0 copy-done.5
  7.5 0.0 copy-start.6
  7.5 1.0 copy-done.6
  8.5 0.0 copy-start.7
  8.5 0.7 copy-done.7
  9.2 0.0 copy-start.8
  9.2 0.7 copy-done.8
  9.9 0.0 copy-start.9
  9.9 0.7 copy-done.9
  10.5 0.0 copy-start.10
  10.5 0.7 copy-done.10
  11.2 111.2 %shard_map.136 = f32[1024,256]{1,0:T(8,128)S(1)} custom-call(f32[3,8,4,8,256]{4,3,2,1,0:T(8,128)S(1)} %bitcast.9, s32[3,256]{1,0:T(4,128)S(1)} %copy-done.7, s32[3,256]{1,0:T(4,128)S(1)} %bitcast.10, s32[2,16]{1,0:T(2,128)S(1)} %copy-done.9, s32[2]{0:T(128)S(1)} %copy-done.10, f32[16,256,128]{2,1,0:T(8,128)} %surface.1, f32[4,31]{1,0:T(4,128)S(1)} %copy-done.8, ...), custom_call_target="tpu_custom_call" | custom-call | tf_op jit(solution)/shard_map/pallas_call | solution.py:495
  122.4 49.8 %all_to_all.5 = f32[128,8,256]{2,1,0:T(8,128)S(1)} all-to-all(f32[128,8,256]{2,1,0:T(8,128)S(1)} %bitcast.8), channel_id=1, replica_groups=mesh['shot'=128,'freq'=4] {'shot'}, dimensions={0} | all-to-all | bytes 2097152 | tf_op jit(solution)/shard_map/all_to_all | solution.py:565
  172.2 0.6 reshape.18
  172.8 0.4 copy.19
  173.2 1.7 reshape.19
Async XLA Ops:
  0.7 1.3 copy-start
  2.0 1.3 copy-start.1
  3.3 1.1 copy-start.2
  4.5 1.0 copy-start.3
  5.5 1.0 copy-start.4
  6.5 1.0 copy-start.5
  7.5 1.0 copy-start.6
  8.5 0.7 copy-start.7
  9.2 0.7 copy-start.8
  9.9 0.7 copy-start.9
  10.5 0.7 copy-start.10

commit v3 on v2

--- a/solution.py
+++ b/solution.py
@@ -110,13 +110,15 @@
 
 
 def spread_kernel(
-    traces, live, bins, cols, owner, surface, filters,
-    wave_all, edge_hi_all, edge_lo_all, combine_hi_all, combine_lo_all, tap_hi, tap_lo,
+    traces_in, live_in, bins_in, cols, owner, surface, filters_in,
+    wave_all, edge_hi_all, edge_lo_all, combine_hi_all, combine_lo_all, tap_hi_in, tap_lo_in,
     packed,
+    traces, live, bins, filters, tap_hi, tap_lo,
     bands, table, wave, edge_hi, edge_lo, combine_hi, combine_lo,
+    out_edge_hi, out_edge_lo, out_combine_hi, out_combine_lo, part_out, part_in,
     onehot, factor, cleaned, clean_hi, clean_lo, slots, rows8, bin_col, live_col, filt, f1x,
     r1, m, r2, hown, hin, ag, specp, specr, specall, sa, sb, srot, pred, f1, f1c,
-    s1s, s1r, s2s, s2r, hs, hr, gs, gr, bs, br, fs, fr,
+    s1s, s1r, s2s, s2r, hs, hr, gs, gr, bs, br, fs, fr, qs, qr,
     ps, pr, cs, cr, u1s, u1r, u2s, u2r, us, ur, own, consts,
 ):
     x, z, h, c, f = place()
@@ -135,6 +137,21 @@
         return o, (shot_of(x, z, h, c), o)
 
     other_h = (shot_of(x, z, 1 - h, c), f)
+
+    inner = (f == 1) | (f == 2)
+    outer = jnp.where(f < 2, 0, NQ - 1)
+    inside = jnp.where(f < 2, 1, 2)
+    pairs = (
+        (filters_in, filters), (live_in, live), (bins_in, bins), (traces_in, traces),
+        (wave_all.at[f], wave), (tap_hi_in, tap_hi), (tap_lo_in, tap_lo),
+        (edge_hi_all.at[f], edge_hi), (edge_lo_all.at[f], edge_lo),
+        (combine_hi_all.at[f], combine_hi), (combine_lo_all.at[f], combine_lo),
+        (edge_hi_all.at[outer], out_edge_hi), (edge_lo_all.at[outer], out_edge_lo),
+        (combine_hi_all.at[outer], out_combine_hi), (combine_lo_all.at[outer], out_combine_lo),
+    )
+    held = [pltpu.make_async_copy(a, b, consts.at[i]) for i, (a, b) in enumerate(pairs)]
+    for one in held:
+        one.start()
 
     barrier = pltpu.get_barrier_semaphore()
 
@@ -184,11 +201,20 @@
             pred.at[p, :, k], bands.at[f, :, at(p), k], bs.at[k, p], br.at[k, at(p)], dev
         )
 
-    def sixth(k, j, at):
-        o, dev = dev_f(j)
+    beside = (shot_of(x, z, h, c), jnp.where(inner, NQ - 1 - f, inside))
+    mate = (shot_of(x, z, h, c), NQ - 1 - f)
+    edge_dev = (shot_of(x, z, h, c), outer)
+
+    def sixth(k, o):
+        return remote(bands.at[f, :, :, k], bands.at[o, :, :, k], fs.at[k, 0], fr.at[k, o], beside)
+
+    def relay(k):
         return remote(
-            bands.at[f, :, :, k], bands.at[at(o), :, :, k], fs.at[k, o], fr.at[k, at(o)], dev
+            bands.at[outer, :, :, k], bands.at[outer, :, :, k], fs.at[k, 1], fr.at[k, outer], mate
         )
+
+    def partial_sum(k):
+        return remote(part_out.at[k], part_in.at[k], qs.at[k], qr.at[k], edge_dev)
 
     def spec_f(j, at):
         o, dev = dev_f(j)
@@ -222,6 +248,7 @@
         return o
 
     filt[...] = jnp.zeros((SUB, 128), F32)
+    held[0].wait()
     filt[0:4, 0:TAPS] = filters[...]
     each(PIECES, lambda j: filt_p(j, to_p).start())
 
@@ -237,16 +264,6 @@
 
     for k in range(CHUNKS):
         own_piece(k).start()
-
-    held = [
-        pltpu.make_async_copy(whole.at[f], part, consts.at[i])
-        for i, (whole, part) in enumerate((
-            (wave_all, wave), (edge_hi_all, edge_hi), (edge_lo_all, edge_lo),
-            (combine_hi_all, combine_hi), (combine_lo_all, combine_lo),
-        ))
-    ]
-    for one in held:
-        one.start()
 
     weights = []
     for b in range(STEPS):
@@ -265,7 +282,8 @@
         for j in range(POINTS_BLK):
             row = b * POINTS_BLK + j
             onehot[row : row + 1, :] = jnp.where(lane_row == cols[b, j], 1.0, 0.0)
-    held[0].wait()
+    for one in held[1:5]:
+        one.wait()
     picked = []
     for s in range(SHOTS):
         pick = onehot[...] * live[s : s + 1, :].astype(F32)
@@ -281,57 +299,69 @@
         specp[o] = part[:, o * LANES : (o + 1) * LANES]
     each(NQ, lambda j: spec_f(j, to_f).start())
     specr[f] = specp[f]
-
     f1[mine] = filt[...]
-    each(PIECES, lambda j: filt_p(j, here).wait_recv())
-    for p in range(PIECES):
-        for i in range(4):
-            f1x[i, p : p + 1, :] = f1[p, i : i + 1, :]
-    lined = f1x[0]
-    for i in range(1, 4):
-        lined = lined + pltpu.roll(f1x[i], i * TAPS, 1)
-    f1c[...] = lined
-    each(NZ, lambda j: filt_z(j, to_z).start())
-
-    each(NQ, lambda j: spec_f(j, here).wait_recv())
-    specall[mine] = specr[0] + specr[1] + specr[2] + specr[3]
-    each(PIECES, lambda j: spec_p(j, to_p).start())
-
-    table[h, z] = f1c[...]
-    each(NZ, lambda j: filt_z(j, here).wait_recv())
-    filt_h(h).start()
-
-    rows8[...] = jnp.zeros((SUB, R), I32)
-    rows8[0:SHOTS, :] = bins[...]
-    rows8[SHOTS : 2 * SHOTS, :] = live[...]
-    turned_rows = rows8[...].T
-    for s in range(SHOTS):
-        bin_col[s] = turned_rows[:, s : s + 1].reshape(PIECES, CHUNKS, SUB, 1)
-        live_col[s] = turned_rows[:, SHOTS + s : SHOTS + s + 1].reshape(PIECES, CHUNKS, SUB, 1)
-    for s in range(SHOTS):
-        row = bins[s : s + 1, :]
-        count = jnp.zeros((1, R), I32)
-        for o in range(s + 1):
-            hit = jnp.where(turned_rows[:, o : o + 1] == row, 1, 0)
-            if o == s:
-                before = lax.broadcasted_iota(I32, (R, R), 0) < lax.broadcasted_iota(
-                    I32, (R, R), 1
-                )
-                hit = jnp.where(before, hit, 0)
-            count = count + jnp.sum(hit, axis=0, keepdims=True)
-        slots[:, s * R : (s + 1) * R] = row * 2 + count
-
-    each(PIECES, lambda j: spec_p(j, here).wait_recv())
-    low = lax.broadcasted_iota(jnp.int32, (SHOTS * COLS, LANES), 1) < BAND
-
-    def both(p, _):
-        v = specall[p]
-        w = pltpu.roll(v, BAND, 1)
-        sa[p] = jnp.where(low, v, w)
-        sb[p] = jnp.where(low, -w, v)
-        return 0
-
-    lax.fori_loop(0, PIECES, both, 0)
+
+    def filters_one():
+        each(PIECES, lambda j: filt_p(j, here).wait_recv())
+        for p in range(PIECES):
+            for i in range(4):
+                f1x[i, p : p + 1, :] = f1[p, i : i + 1, :]
+        lined = f1x[0]
+        for i in range(1, 4):
+            lined = lined + pltpu.roll(f1x[i], i * TAPS, 1)
+        f1c[...] = lined
+        each(NZ, lambda j: filt_z(j, to_z).start())
+        table[h, z] = f1c[...]
+
+    def filters_two():
+        each(NZ, lambda j: filt_z(j, here).wait_recv())
+        filt_h(h).start()
+
+    def filters_three():
+        filt_h(1 - h).wait_recv()
+        for one in held[5:]:
+            one.wait()
+
+    def spectra_one():
+        each(NQ, lambda j: spec_f(j, here).wait_recv())
+        specall[mine] = specr[0] + specr[1] + specr[2] + specr[3]
+        each(PIECES, lambda j: spec_p(j, to_p).start())
+
+    def spectra_two():
+        each(PIECES, lambda j: spec_p(j, here).wait_recv())
+        low = lax.broadcasted_iota(I32, (SHOTS * COLS, LANES), 1) < BAND
+
+        def both(p, _):
+            v = specall[p]
+            w = pltpu.roll(v, BAND, 1)
+            sa[p] = jnp.where(low, v, w)
+            sb[p] = jnp.where(low, -w, v)
+            return 0
+
+        lax.fori_loop(0, PIECES, both, 0)
+
+    def ranks():
+        rows8[...] = jnp.zeros((SUB, R), I32)
+        rows8[0:SHOTS, :] = bins[...].reshape(SHOTS, R)
+        rows8[SHOTS : 2 * SHOTS, :] = live[...]
+        turned_rows = rows8[...].T
+        for s in range(SHOTS):
+            bin_col[s] = turned_rows[:, s : s + 1].reshape(PIECES, CHUNKS, SUB, 1)
+            live_col[s] = turned_rows[:, SHOTS + s : SHOTS + s + 1].reshape(
+                PIECES, CHUNKS, SUB, 1
+            )
+        for s in range(SHOTS):
+            row = bins[s]
+            count = jnp.zeros((1, R), I32)
+            for o in range(s + 1):
+                hit = jnp.where(turned_rows[:, o : o + 1] == row, 1, 0)
+                if o == s:
+                    before = lax.broadcasted_iota(I32, (R, R), 0) < lax.broadcasted_iota(
+                        I32, (R, R), 1
+                    )
+                    hit = jnp.where(before, hit, 0)
+                count = count + jnp.sum(hit, axis=0, keepdims=True)
+            slots[:, s * R : (s + 1) * R] = row * 2 + count
 
     def predict(k):
         each(NZ, lambda j: fourth(k, j, here).wait_recv())
@@ -375,7 +405,7 @@
 
     def gather(k):
         each(PIECES, lambda j: fifth(k, j, here).wait_recv())
-        each(NQ, lambda j: sixth(k, j, to_f).start())
+        sixth(k, f).start()
 
     def across(k):
         each(NZ, lambda j: second(k, j, here).wait_recv())
@@ -409,48 +439,92 @@
         four = dot(pick, top) + (dot(pick, middle) + dot(pick, last))
         start = (one & 3) * TAPS
         four = jnp.where((lane >= start) & (lane < start + TAPS), four, 0.0)
-        factor[k] = dot3(four, tap_hi[...], tap_lo[...])
+        answer = dot3(four, tap_hi[...], tap_lo[...])
+        for o in range(2 * (NQ + 1)):
+            factor[k, o] = answer[:, o * LANES : (o + 1) * LANES]
+
+    def filtered(k, order, e_hi, e_lo, c_hi, c_lo):
+        ends = jnp.zeros((tile, 128), F32)
+        total = jnp.zeros((tile, QUARTER), F32)
+
+        def mix(block, o, span):
+            mixed = block * factor[k, o] + pltpu.roll(block, BAND, 1) * factor[k, NQ + 1 + o]
+            return dot3(mixed, c_hi[span, :], c_lo[span, :])
+
+        for o in order:
+            span = pl.ds(pl.multiple_of(o * LANES, LANES), LANES)
+            block = bands[o, :, :, k].reshape(tile, LANES)
+            ends = ends + dot3(block, e_hi[span, :], e_lo[span, :])
+            total = total + mix(block, o, span)
+        return total + mix(ends, NQ, slice(NQ * LANES, (NQ + 1) * LANES))
+
+    def hand_on(k):
+        @pl.when(inner)
+        def _():
+            sixth(k, outer).wait_recv()
+            relay(k).start()
+
+    def reduce_edge(k):
+        @pl.when(inner)
+        def _():
+            sixth(k, NQ - 1 - f).wait_recv()
+            sixth(k, NQ - 1 - outer).wait_recv()
+            part_out[k] = filtered(
+                k, (f, NQ - 1 - f, NQ - 1 - outer),
+                out_edge_hi, out_edge_lo, out_combine_hi, out_combine_lo,
+            )
+            partial_sum(k).start()
 
     def clean(k):
-        each(NQ, lambda j: sixth(k, j, here).wait_recv())
-        blocks = [bands[o, :, :, k].reshape(tile, LANES) for o in range(NQ)]
-        ends = jnp.zeros((tile, 128), F32)
-        for o in range(NQ):
-            span = slice(o * LANES, (o + 1) * LANES)
-            ends = ends + dot3(blocks[o], edge_hi[span, :], edge_lo[span, :])
-        blocks.append(ends)
-        total = jnp.zeros((tile, QUARTER), F32)
-        width = (NQ + 1) * LANES
-        for o in range(NQ + 1):
-            span = slice(o * LANES, (o + 1) * LANES)
-            cross = slice(width + o * LANES, width + (o + 1) * LANES)
-            mixed = blocks[o] * factor[k, :, span]
-            mixed = mixed + pltpu.roll(blocks[o], BAND, 1) * factor[k, :, cross]
-            total = total + dot3(mixed, combine_hi[span, :], combine_lo[span, :])
-        alive = live_col[:, :, k].reshape(tile, 1).astype(F32)
-        whole = traces[:, :, k].reshape(tile, QUARTER)
-        cleaned[:, :, k] = (alive * (whole - total)).reshape(SHOTS, PIECES, SUB, QUARTER)
+        def put(total):
+            alive = live_col[:, :, k].reshape(tile, 1).astype(F32)
+            whole = traces[:, :, k].reshape(tile, QUARTER)
+            cleaned[:, :, k] = (alive * (whole - total)).reshape(SHOTS, PIECES, SUB, QUARTER)
+
+        @pl.when(inner)
+        def _():
+            put(filtered(k, range(NQ), edge_hi, edge_lo, combine_hi, combine_lo))
+
+        @pl.when(~inner)
+        def _():
+            mine_part = filtered(k, (f,), edge_hi, edge_lo, combine_hi, combine_lo)
+            partial_sum(k).wait_recv()
+            put(mine_part + part_in[k])
 
     def stage(t, lag, fn):
         @pl.when((t >= lag) & (t < lag + CHUNKS))
         def _():
             fn(t - lag)
 
-    for one in held[1:]:
-        one.wait()
-    filt_h(1 - h).wait_recv()
-
     def tick(t, _):
-        stage(t, 5, clean)
+        stage(t, 0, choose)
+        stage(t, 1, across)
+        stage(t, 2, share)
+        stage(t, 3, predict)
         stage(t, 4, gather)
-        stage(t, 3, predict)
-        stage(t, 2, share)
-        stage(t, 1, across)
-        stage(t, 1, prepare)
-        stage(t, 0, choose)
+        stage(t, 5, hand_on)
+        stage(t, 6, reduce_edge)
+        stage(t, 7, clean)
+
+        @pl.when(t == 0)
+        def _():
+            filters_one()
+            spectra_one()
+            ranks()
+
+        @pl.when(t == 1)
+        def _():
+            filters_two()
+            spectra_two()
+
+        @pl.when(t == 2)
+        def _():
+            filters_three()
+
+        stage(t, 3, prepare)
         return 0
 
-    lax.fori_loop(0, CHUNKS + 5, tick, 0)
+    lax.fori_loop(0, CHUNKS + 7, tick, 0)
 
     top, rest = split(cleaned[...].reshape(ROWS, QUARTER))
     clean_hi[...] = top
@@ -472,7 +546,13 @@
         third(k).wait_send()
         each(NZ, lambda j: fourth(k, j, to_z).wait_send())
         each(PIECES, lambda j: fifth(k, j, to_p).wait_send())
-        each(NQ, lambda j: sixth(k, j, to_f).wait_send())
+        sixth(k, f).wait_send()
+
+        @pl.when(inner)
+        def _():
+            relay(k).wait_send()
+            partial_sum(k).wait_send()
+
         return 0
 
     lax.fori_loop(0, CHUNKS, finish, 0)
@@ -495,16 +575,23 @@
     return pl.pallas_call(
         spread_kernel,
         out_shape=jax.ShapeDtypeStruct((1024, QUARTER), F32),
-        in_specs=[vm, vm, vm, sm, sm, hbm, vm, hbm, hbm, hbm, hbm, hbm, vm, vm],
+        in_specs=[hbm, hbm, hbm, sm, sm] + [hbm] * 9,
         out_specs=vm,
         scratch_shapes=[
+            v((SHOTS, PIECES, CHUNKS, SUB, QUARTER), F32),
+            v((SHOTS, R), I32), v((SHOTS, 1, R), I32), v((4, TAPS), F32),
+            v((128, 2 * wide), B16), v((128, 2 * wide), B16),
             v((NQ, SHOTS, PIECES, CHUNKS, *tile), F32),
             v((NH, NZ, PIECES, 128), F32),
             v((QUARTER, NQ * LANES), F32),
             v((NQ * LANES, 128), B16), v((NQ * LANES, 128), B16),
             v((wide, QUARTER), B16), v((wide, QUARTER), B16),
+            v((NQ * LANES, 128), B16), v((NQ * LANES, 128), B16),
+            v((wide, QUARTER), B16), v((wide, QUARTER), B16),
+            v((CHUNKS, SHOTS * PIECES * SUB, QUARTER), F32),
+            v((CHUNKS, SHOTS * PIECES * SUB, QUARTER), F32),
             v((COLS, R), F32),
-            v((CHUNKS, SHOTS * PIECES * SUB, 2 * wide), F32),
+            v((CHUNKS, 2 * (NQ + 1), SHOTS * PIECES * SUB, LANES), F32),
             v((SHOTS, PIECES, CHUNKS, SUB, QUARTER), F32),
             v((ROWS, QUARTER), B16), v((ROWS, QUARTER), B16),
             v((1, ROWS), I32),
@@ -533,17 +620,18 @@
             dma((CHUNKS,)), dma((CHUNKS,)),
             dma((CHUNKS, NZ)), dma((CHUNKS, NZ)),
             dma((CHUNKS, PIECES)), dma((CHUNKS, PIECES)),
-            dma((CHUNKS, NQ)), dma((CHUNKS, NQ)),
+            dma((CHUNKS, 2)), dma((CHUNKS, NQ)),
+            dma((CHUNKS,)), dma((CHUNKS,)),
             dma((NQ,)), dma((NQ,)),
             dma((PIECES,)), dma((PIECES,)),
             dma((PIECES,)), dma((PIECES,)),
             dma((NZ,)), dma((NZ,)),
             dma, dma,
             dma((CHUNKS,)),
-            dma((5,)),
+            dma((15,)),
         ],
         compiler_params=pltpu.CompilerParams(
-            collective_id=0, has_side_effects=True, vmem_limit_bytes=48 * 2**20
+            collective_id=0, has_side_effects=True, vmem_limit_bytes=60 * 2**20
         ),
     )(*args)
 
@@ -552,7 +640,7 @@
     packed = spread(
         traces.reshape(SHOTS, PIECES, CHUNKS, SUB, QUARTER),
         live_mask,
-        offset_bin.reshape(SHOTS, R),
+        offset_bin.reshape(SHOTS, 1, R),
         point_column,
         block_owner,
         surface,

time: 175 us -> 142 us (0.81)
  the two profiles are of different devices: /device:TPU:9 before, /device:TPU:1 now
where the time goes in v3:
time: 142 us; the launch traced here: 141 us
  Pallas kernels  95.4 us (67%)
  blocking collectives  42.9 us (30%)
  local copies, waits for them, and re-layouts  2.67 us (2%)
    pallas_call x1, Pallas kernels, spread(): pl.pallas_call(spread_kernel, out_shape=jax.ShapeDtypeStruct((1024, QUART...  95.4 us
    all_to_all x1, blocking collectives, on_device(): lax.all_to_all(packed, 'shot', split_axis=0, concat_axis=0, tiled=True)  42.9 us

profile of v3, /device:TPU:1, one launch (start us, length us, event | category | flops | bytes accessed | tf_op | source)
XLA Modules:
  0.0 140.9 jit_solution(14717395738303149803)
XLA Ops:
  0.0 95.4 %shard_map.136 = f32[1024,256]{1,0:T(8,128)} custom-call(f32[3,8,4,8,256]{4,3,2,1,0:T(8,128)} %bitcast.8, s32[3,256]{1,0:T(4,128)} %live_in.1, s32[3,1,256]{2,1,0:T(1,128)} %bitcast.9, s32[2,16]{1,0:T(2,128)} %cols.1, s32[2]{0:T(128)} %owner.1, f32[16,256,128]{2,1,0:T(8,128)} %surface.1, f32[4,31]{1,0:T(4,128)} %filters_in.1, ...), custom_call_target="tpu_custom_call" | custom-call | tf_op jit(solution)/shard_map/pallas_call | solution.py:575
  95.4 42.9 %all_to_all.5 = f32[128,8,256]{2,1,0:T(8,128)S(1)} all-to-all(f32[128,8,256]{2,1,0:T(8,128)} %bitcast.6), channel_id=1, replica_groups=mesh['shot'=128,'freq'=4] {'shot'}, dimensions={0} | all-to-all | bytes 2097152 | tf_op jit(solution)/shard_map/all_to_all | solution.py:653
  138.2 0.6 reshape.18
  138.9 0.4 copy.17
  139.2 1.7 %reshape.19 = f32[4,256,256]{2,1,0:T(8,128)} reshape(f32[4,128,2,256]{3,2,1,0:T(2,128)S(1)} %bitcast.7) | data formatting | bytes 2097152 | tf_op jit(solution)/shard_map/reshape | solution.py:655

commit v4 on v3

--- a/solution.py
+++ b/solution.py
@@ -19,6 +19,7 @@
 QUARTER = NT // NQ
 R = 256
 SHOTS = 3
+SHARDS = NX * NZ * NH * NC
 ROWS = SHOTS * R
 PIECES = NX * NC
 CHUNKS = 4
@@ -112,14 +113,14 @@
 def spread_kernel(
     traces_in, live_in, bins_in, cols, owner, surface, filters_in,
     wave_all, edge_hi_all, edge_lo_all, combine_hi_all, combine_lo_all, tap_hi_in, tap_lo_in,
-    packed,
-    traces, live, bins, filters, tap_hi, tap_lo,
+    arrive,
+    packed, traces, live, bins, filters, tap_hi, tap_lo,
     bands, table, wave, edge_hi, edge_lo, combine_hi, combine_lo,
     out_edge_hi, out_edge_lo, out_combine_hi, out_combine_lo, part_out, part_in,
     onehot, factor, cleaned, clean_hi, clean_lo, slots, rows8, bin_col, live_col, filt, f1x,
     r1, m, r2, hown, hin, ag, specp, specr, specall, sa, sb, srot, pred, f1, f1c,
     s1s, s1r, s2s, s2r, hs, hr, gs, gr, bs, br, fs, fr, qs, qr,
-    ps, pr, cs, cr, u1s, u1r, u2s, u2r, us, ur, own, consts,
+    ps, pr, cs, cr, u1s, u1r, u2s, u2r, us, ur, own, consts, ds, dr,
 ):
     x, z, h, c, f = place()
     mine = x * NC + c
@@ -202,15 +203,15 @@
         )
 
     beside = (shot_of(x, z, h, c), jnp.where(inner, NQ - 1 - f, inside))
-    mate = (shot_of(x, z, h, c), NQ - 1 - f)
+    beyond = (shot_of(x, z, h, c), NQ - 1 - inside)
     edge_dev = (shot_of(x, z, h, c), outer)
 
     def sixth(k, o):
         return remote(bands.at[f, :, :, k], bands.at[o, :, :, k], fs.at[k, 0], fr.at[k, o], beside)
 
-    def relay(k):
+    def farther(k):
         return remote(
-            bands.at[outer, :, :, k], bands.at[outer, :, :, k], fs.at[k, 1], fr.at[k, outer], mate
+            bands.at[f, :, :, k], bands.at[f, :, :, k], fs.at[k, 1], fr.at[k, f], beyond
         )
 
     def partial_sum(k):
@@ -246,17 +247,17 @@
 
     def here(o):
         return o
+
+    def start_first(k, _):
+        each(PIECES, lambda j: first(k, j, to_p).start())
+        return 0
+
+    lax.fori_loop(0, CHUNKS, start_first, 0)
 
     filt[...] = jnp.zeros((SUB, 128), F32)
     held[0].wait()
     filt[0:4, 0:TAPS] = filters[...]
     each(PIECES, lambda j: filt_p(j, to_p).start())
-
-    def start_first(k, _):
-        each(PIECES, lambda j: first(k, j, to_p).start())
-        return 0
-
-    lax.fori_loop(0, CHUNKS, start_first, 0)
 
     def own_piece(k):
         src = surface.at[:, pl.ds(pl.multiple_of(mine * (CHUNKS * SUB) + k * SUB, SUB), SUB), :]
@@ -405,6 +406,10 @@
 
     def gather(k):
         each(PIECES, lambda j: fifth(k, j, here).wait_recv())
+        @pl.when(~inner)
+        def _():
+            farther(k).start()
+
         sixth(k, f).start()
 
     def across(k):
@@ -458,15 +463,10 @@
             total = total + mix(block, o, span)
         return total + mix(ends, NQ, slice(NQ * LANES, (NQ + 1) * LANES))
 
-    def hand_on(k):
-        @pl.when(inner)
-        def _():
-            sixth(k, outer).wait_recv()
-            relay(k).start()
-
     def reduce_edge(k):
         @pl.when(inner)
         def _():
+            sixth(k, outer).wait_recv()
             sixth(k, NQ - 1 - f).wait_recv()
             sixth(k, NQ - 1 - outer).wait_recv()
             part_out[k] = filtered(
@@ -502,9 +502,8 @@
         stage(t, 2, share)
         stage(t, 3, predict)
         stage(t, 4, gather)
-        stage(t, 5, hand_on)
-        stage(t, 6, reduce_edge)
-        stage(t, 7, clean)
+        stage(t, 5, reduce_edge)
+        stage(t, 6, clean)
 
         @pl.when(t == 0)
         def _():
@@ -524,21 +523,39 @@
         stage(t, 3, prepare)
         return 0
 
-    lax.fori_loop(0, CHUNKS + 7, tick, 0)
+    lax.fori_loop(0, CHUNKS + 6, tick, 0)
 
     top, rest = split(cleaned[...].reshape(ROWS, QUARTER))
     clean_hi[...] = top
     clean_lo[...] = rest
 
+    me = shot_of(x, z, h, c)
+    group = 128 // SUB
+
+    def deal(t):
+        return remote(packed.at[t], arrive.at[me], ds, dr, (t, f))
+
     def place_rows(i, _):
-        ids = lax.broadcasted_iota(I32, (128, ROWS), 0) + i * 128
+        g = lax.rem(me // group + i, SHARDS // group)
+        ids = lax.broadcasted_iota(I32, (128, ROWS), 0) + g * 128
         pick = jnp.where(ids == slots[...], 1.0, 0.0).astype(B16)
-        packed[pl.ds(pl.multiple_of(i * 128, 128), 128), :] = dot(pick, clean_hi[...]) + dot(
-            pick, clean_lo[...]
-        )
+        block = dot(pick, clean_hi[...]) + dot(pick, clean_lo[...])
+        packed[pl.ds(g * group, group)] = block.reshape(group, SUB, QUARTER)
+
+        def send(j, _):
+            t = g * group + lax.rem(me + j, group)
+
+            @pl.when(t != me)
+            def _():
+                deal(t).start()
+
+            return 0
+
+        lax.fori_loop(0, group, send, 0)
         return 0
 
-    lax.fori_loop(0, packed.shape[0] // 128, place_rows, 0)
+    lax.fori_loop(0, SHARDS // group, place_rows, 0)
+    arrive[me] = packed[me]
 
     def finish(k, _):
         each(PIECES, lambda j: first(k, j, to_p).wait_send())
@@ -548,9 +565,12 @@
         each(PIECES, lambda j: fifth(k, j, to_p).wait_send())
         sixth(k, f).wait_send()
 
+        @pl.when(~inner)
+        def _():
+            farther(k).wait_send()
+
         @pl.when(inner)
         def _():
-            relay(k).wait_send()
             partial_sum(k).wait_send()
 
         return 0
@@ -561,6 +581,9 @@
     each(PIECES, lambda j: filt_p(j, to_p).wait_send())
     each(NZ, lambda j: filt_z(j, to_z).wait_send())
     filt_h(h).wait_send()
+    others = pl.ds(0, SHARDS - 1)
+    pltpu.make_async_copy(packed.at[others], packed.at[others], ds).wait()
+    pltpu.make_async_copy(arrive.at[others], arrive.at[others], dr).wait()
 
 
 def spread(*args):
@@ -574,10 +597,11 @@
     wide = (NQ + 1) * LANES
     return pl.pallas_call(
         spread_kernel,
-        out_shape=jax.ShapeDtypeStruct((1024, QUARTER), F32),
+        out_shape=jax.ShapeDtypeStruct((SHARDS, SUB, QUARTER), F32),
         in_specs=[hbm, hbm, hbm, sm, sm] + [hbm] * 9,
         out_specs=vm,
         scratch_shapes=[
+            v((SHARDS, SUB, QUARTER), F32),
             v((SHOTS, PIECES, CHUNKS, SUB, QUARTER), F32),
             v((SHOTS, R), I32), v((SHOTS, 1, R), I32), v((4, TAPS), F32),
             v((128, 2 * wide), B16), v((128, 2 * wide), B16),
@@ -629,6 +653,7 @@
             dma, dma,
             dma((CHUNKS,)),
             dma((15,)),
+            dma, dma,
         ],
         compiler_params=pltpu.CompilerParams(
             collective_id=0, has_side_effects=True, vmem_limit_bytes=60 * 2**20
@@ -637,7 +662,7 @@
 
 
 def on_device(traces, live_mask, offset_bin, surface, block_owner, point_column, filters):
-    packed = spread(
+    dealt = spread(
         traces.reshape(SHOTS, PIECES, CHUNKS, SUB, QUARTER),
         live_mask,
         offset_bin.reshape(SHOTS, 1, R),
@@ -649,9 +674,7 @@
         jnp.asarray(TAP_HI),
         jnp.asarray(TAP_LO),
     )
-    packed = packed.reshape(128, 8, QUARTER)
-    dealt = lax.all_to_all(packed, "shot", split_axis=0, concat_axis=0, tiled=True)
-    dealt = dealt.reshape(128, 4, 2, QUARTER).transpose(1, 0, 2, 3)
+    dealt = dealt.reshape(SHARDS, 4, 2, QUARTER).transpose(1, 0, 2, 3)
     return dealt.reshape(4, 256, QUARTER)
 
 

time: 142 us -> 127 us (0.89)
  blocking collectives: 42.9 us -> 0 us
  Pallas kernels: 95.4 us -> 123 us
    all_to_all x1 -> x0, blocking collectives: 42.9 us -> none  [on_device(): lax.all_to_all(packed, 'shot', split_axis=0, concat_axis=0, tiled=True)]
    pallas_call x1, Pallas kernels: 95.4 us -> 123 us  [spread(): pl.pallas_call(spread_kernel, out_shape=jax.ShapeDtypeStruct((SHARDS, SUB...]
where the time goes in v4:
time: 127 us
  Pallas kernels  123 us (97%)
  local copies, waits for them, and re-layouts  3.9 us (3%)
    pallas_call x1, Pallas kernels, spread(): pl.pallas_call(spread_kernel, out_shape=jax.ShapeDtypeStruct((SHARDS, SUB...  123 us

profile of v4, /device:TPU:1, one launch (start us, length us, event | category | flops | bytes accessed | tf_op | source)
XLA Modules:
  0.0 126.9 jit_solution(1492945521234615768)
XLA Ops:
  0.0 123.0 %shard_map.136 = f32[128,8,256]{2,1,0:T(8,128)} custom-call(f32[3,8,4,8,256]{4,3,2,1,0:T(8,128)} %bitcast.4, s32[3,256]{1,0:T(4,128)} %live_in.1, s32[3,1,256]{2,1,0:T(1,128)} %bitcast.5, s32[2,16]{1,0:T(2,128)} %cols.1, s32[2]{0:T(128)} %owner.1, f32[16,256,128]{2,1,0:T(8,128)} %surface.1, f32[4,31]{1,0:T(4,128)} %filters_in.1, ...), custom_call_target="tpu_custom_call" | custom-call | tf_op jit(solution)/shard_map/pallas_call | solution.py:598
  123.0 1.8 %reshape.14 = f32[128,4,2,256]{3,2,1,0:T(2,128)S(1)} reshape(f32[128,8,256]{2,1,0:T(8,128)} %shard_map.136) | data formatting | bytes 2097152 | tf_op jit(solution)/shard_map/reshape | solution.py:677
  124.8 0.4 copy.15
  125.2 1.7 %reshape.15 = f32[4,256,256]{2,1,0:T(8,128)} reshape(f32[4,128,2,256]{3,2,1,0:T(2,128)S(1)} %copy.15) | data formatting | bytes 2097152 | tf_op jit(solution)/shard_map/reshape | solution.py:678

commit v5 on v4

--- a/solution.py
+++ b/solution.py
@@ -19,10 +19,12 @@
 QUARTER = NT // NQ
 R = 256
 SHOTS = 3
+MOST = 2
 SHARDS = NX * NZ * NH * NC
 ROWS = SHOTS * R
 PIECES = NX * NC
 CHUNKS = 4
+AHEAD = 2
 SUB = 8
 COLS = STEPS * POINTS_BLK
 PAIR = POINTS_BLK // NZ
@@ -113,8 +115,8 @@
 def spread_kernel(
     traces_in, live_in, bins_in, cols, owner, surface, filters_in,
     wave_all, edge_hi_all, edge_lo_all, combine_hi_all, combine_lo_all, tap_hi_in, tap_lo_in,
-    arrive,
-    packed, traces, live, bins, filters, tap_hi, tap_lo,
+    sorted_rows,
+    arrive, packed, traces, live, bins, filters, tap_hi, tap_lo,
     bands, table, wave, edge_hi, edge_lo, combine_hi, combine_lo,
     out_edge_hi, out_edge_lo, out_combine_hi, out_combine_lo, part_out, part_in,
     onehot, factor, cleaned, clean_hi, clean_lo, slots, rows8, bin_col, live_col, filt, f1x,
@@ -252,12 +254,12 @@
         each(PIECES, lambda j: first(k, j, to_p).start())
         return 0
 
-    lax.fori_loop(0, CHUNKS, start_first, 0)
-
     filt[...] = jnp.zeros((SUB, 128), F32)
     held[0].wait()
     filt[0:4, 0:TAPS] = filters[...]
     each(PIECES, lambda j: filt_p(j, to_p).start())
+
+    lax.fori_loop(0, AHEAD, start_first, 0)
 
     def own_piece(k):
         src = surface.at[:, pl.ds(pl.multiple_of(mine * (CHUNKS * SUB) + k * SUB, SUB), SUB), :]
@@ -520,6 +522,10 @@
         def _():
             filters_three()
 
+        @pl.when(t + AHEAD < CHUNKS)
+        def _():
+            start_first(t + AHEAD, 0)
+
         stage(t, 3, prepare)
         return 0
 
@@ -584,6 +590,23 @@
     others = pl.ds(0, SHARDS - 1)
     pltpu.make_async_copy(packed.at[others], packed.at[others], ds).wait()
     pltpu.make_async_copy(arrive.at[others], arrive.at[others], dr).wait()
+    pairs_of = lax.broadcasted_iota(I32, (SUB, QUARTER), 0) // MOST
+
+    def sort_rows(i, _):
+        for b in range(SUB // MOST):
+            total = arrive[4 * i]
+            if b:
+                total = pltpu.roll(total, SUB - MOST * b, 0)
+            for j in range(1, 4):
+                turn = MOST * (j - b) % SUB
+                other = arrive[4 * i + j]
+                if turn:
+                    other = pltpu.roll(other, turn, 0)
+                total = jnp.where(pairs_of == j, other, total)
+            sorted_rows[b, pl.ds(pl.multiple_of(i * SUB, SUB), SUB), :] = total
+        return 0
+
+    lax.fori_loop(0, SHARDS // 4, sort_rows, 0)
 
 
 def spread(*args):
@@ -597,11 +620,11 @@
     wide = (NQ + 1) * LANES
     return pl.pallas_call(
         spread_kernel,
-        out_shape=jax.ShapeDtypeStruct((SHARDS, SUB, QUARTER), F32),
+        out_shape=jax.ShapeDtypeStruct((SUB // MOST, SHARDS * MOST, QUARTER), F32),
         in_specs=[hbm, hbm, hbm, sm, sm] + [hbm] * 9,
         out_specs=vm,
         scratch_shapes=[
-            v((SHARDS, SUB, QUARTER), F32),
+            v((SHARDS, SUB, QUARTER), F32), v((SHARDS, SUB, QUARTER), F32),
             v((SHOTS, PIECES, CHUNKS, SUB, QUARTER), F32),
             v((SHOTS, R), I32), v((SHOTS, 1, R), I32), v((4, TAPS), F32),
             v((128, 2 * wide), B16), v((128, 2 * wide), B16),
@@ -662,7 +685,7 @@
 
 
 def on_device(traces, live_mask, offset_bin, surface, block_owner, point_column, filters):
-    dealt = spread(
+    return spread(
         traces.reshape(SHOTS, PIECES, CHUNKS, SUB, QUARTER),
         live_mask,
         offset_bin.reshape(SHOTS, 1, R),
@@ -674,8 +697,6 @@
         jnp.asarray(TAP_HI),
         jnp.asarray(TAP_LO),
     )
-    dealt = dealt.reshape(SHARDS, 4, 2, QUARTER).transpose(1, 0, 2, 3)
-    return dealt.reshape(4, 256, QUARTER)
 
 
 def solution(mesh):

time: 127 us -> 117 us (0.921)
  Pallas kernels: 123 us -> 115 us
  local copies, waits for them, and re-layouts: 3.9 us -> 2.29 us
    pallas_call x1, Pallas kernels: 123 us -> 115 us  [spread(): pl.pallas_call(spread_kernel, out_shape=jax.ShapeDtypeStruct((SUB // MOST...]
    reshape x2 -> x0, local copies, waits for them, and re-layouts: 3.53 us -> none  [the longest x1 1.84 us: on_device(): dealt = dealt.reshape(SHARDS, 4, 2, QUARTER).transpose(1, 0, 2, 3)]
    unnamed x0 -> x1, local copies, waits for them, and re-layouts: none -> 2.29 us
where the time goes in v5:
time: 117 us
  Pallas kernels  115 us (98%)
  local copies, waits for them, and re-layouts  2.29 us (2%)
    pallas_call x1, Pallas kernels, spread(): pl.pallas_call(spread_kernel, out_shape=jax.ShapeDtypeStruct((SUB // MOST...  115 us

profile of v5, /device:TPU:1, one launch (start us, length us, event | category | flops | bytes accessed | tf_op | source)
XLA Modules:
  0.0 117.0 jit_solution(1306436258070102401)
XLA Ops:
  0.0 114.7 %shard_map.136 = f32[4,256,256]{2,1,0:T(8,128)} custom-call(f32[3,8,4,8,256]{4,3,2,1,0:T(8,128)} %bitcast.2, s32[3,256]{1,0:T(4,128)} %live_in.1, s32[3,1,256]{2,1,0:T(1,128)} %bitcast.3, s32[2,16]{1,0:T(2,128)} %cols.1, s32[2]{0:T(128)} %owner.1, f32[16,256,128]{2,1,0:T(8,128)} %surface.1, f32[4,31]{1,0:T(4,128)} %filters_in.1, ...), custom_call_target="tpu_custom_call" | custom-call | tf_op jit(solution)/shard_map/pallas_call | solution.py:621
  114.8 2.3 %copy.16 = f32[4,256,256]{2,1,0:T(8,128)} copy(f32[4,256,256]{2,1,0:T(8,128)} %shard_map.136) | data formatting | bytes 2097152

commit v6 on v5

--- a/solution.py
+++ b/solution.py
@@ -254,12 +254,13 @@
         each(PIECES, lambda j: first(k, j, to_p).start())
         return 0
 
+    start_first(0, 0)
     filt[...] = jnp.zeros((SUB, 128), F32)
     held[0].wait()
     filt[0:4, 0:TAPS] = filters[...]
     each(PIECES, lambda j: filt_p(j, to_p).start())
 
-    lax.fori_loop(0, AHEAD, start_first, 0)
+    lax.fori_loop(1, AHEAD, start_first, 0)
 
     def own_piece(k):
         src = surface.at[:, pl.ds(pl.multiple_of(mine * (CHUNKS * SUB) + k * SUB, SUB), SUB), :]
@@ -539,7 +540,7 @@
     group = 128 // SUB
 
     def deal(t):
-        return remote(packed.at[t], arrive.at[me], ds, dr, (t, f))
+        return remote(packed.at[t], arrive.at[me], ds, dr.at[me // group], (t, f))
 
     def place_rows(i, _):
         g = lax.rem(me // group + i, SHARDS // group)
@@ -587,26 +588,44 @@
     each(PIECES, lambda j: filt_p(j, to_p).wait_send())
     each(NZ, lambda j: filt_z(j, to_z).wait_send())
     filt_h(h).wait_send()
-    others = pl.ds(0, SHARDS - 1)
-    pltpu.make_async_copy(packed.at[others], packed.at[others], ds).wait()
-    pltpu.make_async_copy(arrive.at[others], arrive.at[others], dr).wait()
     pairs_of = lax.broadcasted_iota(I32, (SUB, QUARTER), 0) // MOST
 
-    def sort_rows(i, _):
-        for b in range(SUB // MOST):
-            total = arrive[4 * i]
-            if b:
-                total = pltpu.roll(total, SUB - MOST * b, 0)
-            for j in range(1, 4):
-                turn = MOST * (j - b) % SUB
-                other = arrive[4 * i + j]
-                if turn:
-                    other = pltpu.roll(other, turn, 0)
-                total = jnp.where(pairs_of == j, other, total)
-            sorted_rows[b, pl.ds(pl.multiple_of(i * SUB, SUB), SUB), :] = total
+    def came(g, count):
+        some = arrive.at[pl.ds(0, count)]
+        pltpu.make_async_copy(some, some, dr.at[g]).wait()
+
+    def sort_group(n, _):
+        g = lax.rem(me // group + SHARDS // group - n, SHARDS // group)
+
+        @pl.when(n == 0)
+        def _():
+            came(g, group - 1)
+
+        @pl.when(n != 0)
+        def _():
+            came(g, group)
+
+        def sort_rows(s, _):
+            i = g * (group // 4) + s
+            for b in range(SUB // MOST):
+                total = arrive[4 * i]
+                if b:
+                    total = pltpu.roll(total, SUB - MOST * b, 0)
+                for j in range(1, 4):
+                    turn = MOST * (j - b) % SUB
+                    other = arrive[4 * i + j]
+                    if turn:
+                        other = pltpu.roll(other, turn, 0)
+                    total = jnp.where(pairs_of == j, other, total)
+                sorted_rows[b, pl.ds(pl.multiple_of(i * SUB, SUB), SUB), :] = total
+            return 0
+
+        lax.fori_loop(0, group // 4, sort_rows, 0)
         return 0
 
-    lax.fori_loop(0, SHARDS // 4, sort_rows, 0)
+    lax.fori_loop(0, SHARDS // group, sort_group, 0)
+    others = packed.at[pl.ds(0, SHARDS - 1)]
+    pltpu.make_async_copy(others, others, ds).wait()
 
 
 def spread(*args):
@@ -676,7 +695,7 @@
             dma, dma,
             dma((CHUNKS,)),
             dma((15,)),
-            dma, dma,
+            dma, dma((8,)),
         ],
         compiler_params=pltpu.CompilerParams(
             collective_id=0, has_side_effects=True, vmem_limit_bytes=60 * 2**20

time: 117 us -> 117 us (level)
  no operation moved by 1% of the time
where the time goes in v6:
time: 117 us
  Pallas kernels  114 us (97%)
  local copies, waits for them, and re-layouts  2.29 us (2%)
    pallas_call x1, Pallas kernels, spread(): pl.pallas_call(spread_kernel, out_shape=jax.ShapeDtypeStruct((SUB // MOST...  114 us

profile of v6, /device:TPU:1, one launch (start us, length us, event | category | flops | bytes accessed | tf_op | source)
XLA Modules:
  0.0 116.6 jit_solution(5424742616751531803)
XLA Ops:
  0.0 114.3 %shard_map.136 = f32[4,256,256]{2,1,0:T(8,128)} custom-call(f32[3,8,4,8,256]{4,3,2,1,0:T(8,128)} %bitcast.2, s32[3,256]{1,0:T(4,128)} %live_in.1, s32[3,1,256]{2,1,0:T(1,128)} %bitcast.3, s32[2,16]{1,0:T(2,128)} %cols.1, s32[2]{0:T(128)} %owner.1, f32[16,256,128]{2,1,0:T(8,128)} %surface.1, f32[4,31]{1,0:T(4,128)} %filters_in.1, ...), custom_call_target="tpu_custom_call" | custom-call | tf_op jit(solution)/shard_map/pallas_call | solution.py:640
  114.3 2.3 %copy.16 = f32[4,256,256]{2,1,0:T(8,128)} copy(f32[4,256,256]{2,1,0:T(8,128)} %shard_map.136) | data formatting | bytes 2097152

commit v7 on v6

--- a/solution.py
+++ b/solution.py
@@ -501,12 +501,11 @@
 
     def tick(t, _):
         stage(t, 0, choose)
-        stage(t, 1, across)
-        stage(t, 2, share)
-        stage(t, 3, predict)
-        stage(t, 4, gather)
-        stage(t, 5, reduce_edge)
-        stage(t, 6, clean)
+        stage(t, 1, share)
+        stage(t, 2, predict)
+        stage(t, 3, gather)
+        stage(t, 4, reduce_edge)
+        stage(t, 5, clean)
 
         @pl.when(t == 0)
         def _():
@@ -523,6 +522,8 @@
         def _():
             filters_three()
 
+        stage(t, 0, across)
+
         @pl.when(t + AHEAD < CHUNKS)
         def _():
             start_first(t + AHEAD, 0)
@@ -530,7 +531,7 @@
         stage(t, 3, prepare)
         return 0
 
-    lax.fori_loop(0, CHUNKS + 6, tick, 0)
+    lax.fori_loop(0, CHUNKS + 5, tick, 0)
 
     top, rest = split(cleaned[...].reshape(ROWS, QUARTER))
     clean_hi[...] = top

time: 117 us -> 119 us (1.017)
  Pallas kernels: 114 us -> 117 us
    pallas_call x1, Pallas kernels: 114 us -> 117 us  [spread(): pl.pallas_call(spread_kernel, out_shape=jax.ShapeDtypeStruct((SUB // MOST...]
where the time goes in v7:
time: 119 us
  Pallas kernels  117 us (98%)
  local copies, waits for them, and re-layouts  2.29 us (2%)
    pallas_call x1, Pallas kernels, spread(): pl.pallas_call(spread_kernel, out_shape=jax.ShapeDtypeStruct((SUB // MOST...  117 us

profile of v7, /device:TPU:1, one launch (start us, length us, event | category | flops | bytes accessed | tf_op | source)
XLA Modules:
  0.0 119.2 jit_solution(7806392390006770739)
XLA Ops:
  0.0 116.9 %shard_map.136 = f32[4,256,256]{2,1,0:T(8,128)} custom-call(f32[3,8,4,8,256]{4,3,2,1,0:T(8,128)} %bitcast.2, s32[3,256]{1,0:T(4,128)} %live_in.1, s32[3,1,256]{2,1,0:T(1,128)} %bitcast.3, s32[2,16]{1,0:T(2,128)} %cols.1, s32[2]{0:T(128)} %owner.1, f32[16,256,128]{2,1,0:T(8,128)} %surface.1, f32[4,31]{1,0:T(4,128)} %filters_in.1, ...), custom_call_target="tpu_custom_call" | custom-call | tf_op jit(solution)/shard_map/pallas_call | solution.py:641
  116.9 2.3 %copy.16 = f32[4,256,256]{2,1,0:T(8,128)} copy(f32[4,256,256]{2,1,0:T(8,128)} %shard_map.136) | data formatting | bytes 2097152
